TPU v7x, 768 devices: a whole 4x8x12 slice. The times are simulated.
768 devices in a mesh: lat: 192 (over z, y_hi, x, core), lon: 4 (over y_lo).
Axes of the slice: x: 4, y: 8 (y_hi: 2, y_lo: 4; y = y_hi * 4 + y_lo), z: 12, core: 2. Of those that a mesh axis runs over, the one named last changes fastest.
Arguments:
- lam_end: float32 [4, 16, 1536, 512], P(None, None, 'lat', 'lon'), may hold values from -6 to 6
- winds: float32 [2, 16, 1536, 512], P(None, None, 'lat', 'lon'), may hold values from -0.5 to 0.5
- coupling: float32 [4, 16, 1536, 512], P(None, None, 'lat', 'lon'), may hold values from -0.5 to 0.5
- obs_values: float32 [768, 4, 64, 128], P(('lat', 'lon')), may hold values from -6 to 6
- obs_column: int32 [768, 4, 64], P(('lat', 'lon')), may hold values from 0 to 1023
- obs_count: int32 [768, 4], P(('lat', 'lon')), may hold values from 8 to 64, as said below
Outputs:
- gradient: float32 [4, 16, 1536, 512], P(None, None, 'lat', 'lon')
Inputs may be any that keep to these rules, and one draw needn't show every extreme that they name: `obs_column`: target column of a slot within its destination tile, numbered latitude row times 128 plus longitude column, in the sender's own latitude band; targets may repeat, and padding slots hold targets too. `obs_count`: slots from this count on are padding. In every latitude band some destination tile, drawn from the seed, gets 64 live slots from every device of the band.
All inputs are finite; a program needn't handle non-finite values.
Results may differ from a plain program's by a relative error of at most 0.00002.
Values sent between devices are 32-bit elements; how exact they have to be, the bound alone decides.
No kernel may reach another device: no remote copies, remote signals or barrier semaphores. Data moves between devices by JAX's collectives and lax.ppermute only.
A program may use at most 32 MiB of HBM per device.

v0:
```python
import jax
import jax.numpy as jnp
from jax import lax
from jax.sharding import PartitionSpec as P

DIFFUSION = 0.1


def with_halo(cells, sides, width):
    for axis, dim in sides:
        count = lax.axis_size(axis)
        head = lax.slice_in_dim(cells, 0, width, axis=dim)
        tail = lax.slice_in_dim(cells, cells.shape[dim] - width, cells.shape[dim], axis=dim)
        cells = jnp.concatenate(
            [
                lax.ppermute(tail, axis, [(i, (i + 1) % count) for i in range(count)]),
                cells,
                lax.ppermute(head, axis, [((i + 1) % count, i) for i in range(count)]),
            ],
            axis=dim,
        )
    return cells


def adjoint_step(padded, lat_wind, lon_wind, coupling):
    lat_flux = lat_wind * padded
    lon_flux = lon_wind * padded
    centre = padded[..., 1:-1, 1:-1]
    upper = padded[..., 2:, 1:-1]
    lower = padded[..., :-2, 1:-1]
    right_side = padded[..., 1:-1, 2:]
    left_side = padded[..., 1:-1, :-2]
    advect = 0.5 * (
        lat_flux[..., 2:, 1:-1]
        - lat_flux[..., :-2, 1:-1]
        + lon_flux[..., 1:-1, 2:]
        - lon_flux[..., 1:-1, :-2]
    )
    updated = centre + advect + DIFFUSION * (upper + lower + right_side + left_side - 4.0 * centre)
    couple_centre = coupling[..., 1:-1, 1:-1]
    wind_lat = updated[0] - (couple_centre[0] * centre[2] + couple_centre[2] * centre[3])
    wind_lon = updated[1] - (couple_centre[1] * centre[2] + couple_centre[3] * centre[3])
    return jnp.stack([wind_lat, wind_lon, updated[2], updated[3]])


def pole_mask(rim_width, tile_rows):
    first_row = lax.axis_index("lat") * tile_rows - rim_width
    global_rows = first_row + jnp.arange(tile_rows + 2 * rim_width, dtype=jnp.int32)
    total_rows = tile_rows * lax.axis_size("lat")
    inside = jnp.logical_and(global_rows >= 0, global_rows < total_rows)
    return inside.astype(jnp.float32)[:, None]


def add_forcing(state, force_pair):
    return jnp.concatenate([state[:2], state[2:] + force_pair])


def body(lam_end, winds, coupling, obs_values, obs_column, obs_count):
    levels = lam_end.shape[1]
    tile_rows = lam_end.shape[2]
    tile_cols = lam_end.shape[3]
    lon_tiles = lax.axis_size("lon")
    capacity = obs_values.shape[2]
    block_width = obs_values.shape[3]
    step_count = block_width // (2 * levels)
    slot_ids = jnp.arange(capacity, dtype=jnp.int32)
    live_slots = (slot_ids[None, :] < obs_count[0][:, None]).astype(jnp.float32)
    outgoing = obs_values[0] * live_slots[:, :, None]
    arrived, targets = (
        lax.all_to_all(outgoing, "lon", split_axis=0, concat_axis=0, tiled=True),
        lax.all_to_all(obs_column[0], "lon", split_axis=0, concat_axis=0, tiled=True),
    )
    count_rows = lon_tiles * capacity
    tile_cells = tile_rows * tile_cols
    summed = jax.ops.segment_sum(
        arrived.reshape(count_rows, block_width),
        targets.reshape(count_rows).astype(jnp.int32),
        num_segments=tile_cells,
    )
    forcing = summed.T.reshape(step_count * 2, levels, tile_rows, tile_cols)
    last_slot = step_count - 1
    first_state = add_forcing(lam_end, forcing[2 * last_slot : 2 * last_slot + 2])
    extended = with_halo(
        jnp.concatenate([winds, coupling, first_state], 0), (("lat", 2), ("lon", 3)), 1
    )
    lat_wind = extended[0]
    lon_wind = extended[1]
    couple_ext = extended[2:6]
    edge_mask = pole_mask(1, tile_rows)
    adjoint = first_state
    for instant in range(step_count):
        slot_time = step_count - 1 - instant
        if instant == 0:
            padded = extended[6:10] * edge_mask
        else:
            adjoint = add_forcing(adjoint, forcing[2 * slot_time : 2 * slot_time + 2])
            padded = with_halo(adjoint, (("lat", 2), ("lon", 3)), 1) * edge_mask
        adjoint = adjoint_step(padded, lat_wind, lon_wind, couple_ext)
    return adjoint


def solution(mesh):
    return jax.shard_map(
        body,
        mesh=mesh,
        in_specs=(
            P(None, None, "lat", "lon"),
            P(None, None, "lat", "lon"),
            P(None, None, "lat", "lon"),
            P(("lat", "lon"), None, None, None),
            P(("lat", "lon"), None, None),
            P(("lat", "lon"), None),
        ),
        out_specs=P(None, None, "lat", "lon"),
        check_vma=False,
    )
```

profile of v0, /device:TPU:8, one launch (start us, length us, event | category | flops | bytes accessed | tf_op | source)
XLA Modules:
  0.0 176.8 jit_solution(1278210517130943507)
XLA Ops:
  0.0 12.6 %all-to-all-start = ((s32[4,1,64]{2,1,0:T(1,128)}), s32[4,1,64]{2,1,0:T(1,128)S(1)}, u32[]{:S(2)}, u32[]{:S(2)}) async-start(s32[4,1,64]{2,1,0:T(1,128)} %bitcast.39), calls=%async_computation | async-start | bytes 4096 | tf_op jit(solution)/shard_map/all_to_all | solution.py:71
  12.6 0.7 fusion.22
  13.4 1.7 bitcast_multiply_fusion
  15.0 1.6 all-to-all-done
  16.7 4.7 %all-to-all-start.1 = ((f32[4,64,128]{2,1,0:T(8,128)}), f32[4,64,128]{2,1,0:T(8,128)S(1)}, u32[]{:S(2)}, u32[]{:S(2)}) async-start(f32[4,64,128]{2,1,0:T(8,128)} %bitcast_multiply_fusion), calls=%async_computation.1 | async-start | bytes 262144 | tf_op jit(solution)/shard_map/all_to_all | solution.py:70
  22.7 3.9 %all-to-all-done.1 = f32[4,64,128]{2,1,0:T(8,128)S(1)} async-done(((f32[4,64,128]{2,1,0:T(8,128)}), f32[4,64,128]{2,1,0:T(8,128)S(1)}, u32[]{:S(2)}, u32[]{:S(2)}) %all-to-all-start.1) | async-done | bytes 131104 | tf_op jit(solution)/shard_map/all_to_all | solution.py:70
  26.6 1.5 scatter_custom_fusion
  28.2 1.6 fusion.27
  30.0 0.7 copy-done
  30.8 1.9 %collective-permute-start = (f32[10,16,1,128]{3,2,1,0:T(1,128)S(1)}, f32[10,16,1,128]{3,2,1,0:T(1,128)S(1)}, u32[]{:S(2)}, u32[]{:S(2)}) collective-permute-start(f32[10,16,1,128]{3,2,1,0:T(1,128)S(1)} %get-tuple-element.25), channel_id=1, source_target_pairs={{0,4},{4,8},{8,12},{12,16},{16,20},{20,24},{24,28},{28,32},{32,36}... | collective-permute-start | bytes 245768 | tf_op jit(solution)/shard_map/ppermute | solution.py:16
  32.8 11.8 %collective-permute-start.1 = (f32[10,16,1,128]{3,2,1,0:T(1,128)S(1)}, f32[10,16,1,128]{3,2,1,0:T(1,128)S(1)}, u32[]{:S(2)}, u32[]{:S(2)}) collective-permute-start(f32[10,16,1,128]{3,2,1,0:T(1,128)S(1)} %get-tuple-element.26), channel_id=1, source_target_pairs={{4,0},{8,4},{12,8},{16,12},{20,16},{24,20},{28,24},{32,28},{36,32}... | collective-permute-start | bytes 245768 | tf_op jit(solution)/shard_map/ppermute | solution.py:18
  44.6 0.9 collective-permute-done
  45.5 1.1 collective-permute-done.1
  47.3 1.3 copy.17
  48.6 0.7 copy.18
  49.2 2.7 %collective-permute-start.3 = (f32[10,16,10,1]{1,3,2,0:T(1,128)S(1)}, f32[10,16,10,1]{1,3,2,0:T(1,128)S(1)}, u32[]{:S(2)}, u32[]{:S(2)}) collective-permute-start(f32[10,16,10,1]{1,3,2,0:T(1,128)S(1)} %copy.18), channel_id=1, source_target_pairs={{1,0},{2,1},{3,2},{0,3},{5,4},{6,5},{7,6},{4,7},{9,8},{10,9},{11,1... | collective-permute-start | bytes 19208 | tf_op jit(solution)/shard_map/ppermute | solution.py:18
  51.9 3.2 %collective-permute-start.2 = (f32[10,16,10,1]{1,3,2,0:T(1,128)S(1)}, f32[10,16,10,1]{1,3,2,0:T(1,128)S(1)}, u32[]{:S(2)}, u32[]{:S(2)}) collective-permute-start(f32[10,16,10,1]{1,3,2,0:T(1,128)S(1)} %copy-done.7), channel_id=1, source_target_pairs={{0,1},{1,2},{2,3},{3,0},{4,5},{5,6},{6,7},{7,4},{8,9},{9,10},{10,1... | collective-permute-start | bytes 19208 | tf_op jit(solution)/shard_map/ppermute | solution.py:16
  55.3 2.6 %collective-permute-done.2 = f32[10,16,10,1]{1,3,2,0:T(1,128)S(1)} collective-permute-done((f32[10,16,10,1]{1,3,2,0:T(1,128)S(1)}, f32[10,16,10,1]{1,3,2,0:T(1,128)S(1)}, u32[]{:S(2)}, u32[]{:S(2)}) %collective-permute-start.2) | collective-permute-done | bytes 6432 | tf_op jit(solution)/shard_map/ppermute | solution.py:16
  57.9 0.7 copy.19
  58.7 0.7 copy.20
  59.4 2.6 %pad_maximum_fusion = f32[10,16,10,130]{3,2,1,0:T(8,128)S(1)} fusion(f32[10,16,10,1]{3,2,1,0:T(8,128)S(1)} %copy.20, f32[10,16,1,128]{3,2,1,0:T(1,128)} %copy-done.5, f32[2,16,8,128]{3,2,1,0:T(8,128)S(1)} %get-tuple-element.44, f32[2,16,8,128]{3,2,1,0:T(8,128)S(1)} %get-tuple-element.43, f32[4,16,8,128]{3,2,1,0:T(8,128)S(1)} %copy-done, ...), kind=kLoop, calls=%fused_computation.1 | loop fusion | flops 1456000 | bytes 1664000 | tf_op jit(solution)/shard_map/concatenate | solution.py:14
  63.3 1.9 %collective-permute-start.4 = (f32[4,16,1,128]{3,2,1,0:T(1,128)S(1)}, f32[4,16,1,128]{3,2,1,0:T(1,128)S(1)}, u32[]{:S(2)}, u32[]{:S(2)}) collective-permute-start(f32[4,16,1,128]{3,2,1,0:T(1,128)S(1)} %get-tuple-element.41), channel_id=1, source_target_pairs={{0,4},{4,8},{8,12},{12,16},{16,20},{20,24},{24,28},{28,32},{32,36}... | collective-permute-start | bytes 98312 | tf_op jit(solution)/shard_map/ppermute | solution.py:16
  65.3 11.9 %collective-permute-start.5 = (f32[4,16,1,128]{3,2,1,0:T(1,128)S(1)}, f32[4,16,1,128]{3,2,1,0:T(1,128)S(1)}, u32[]{:S(2)}, u32[]{:S(2)}) collective-permute-start(f32[4,16,1,128]{3,2,1,0:T(1,128)S(1)} %get-tuple-element.42), channel_id=1, source_target_pairs={{4,0},{8,4},{12,8},{16,12},{20,16},{24,20},{28,24},{32,28},{36,32}... | collective-permute-start | bytes 98312 | tf_op jit(solution)/shard_map/ppermute | solution.py:18
  77.2 1.6 collective-permute-done.5
  78.8 1.0 fusion.26
  79.8 3.2 %collective-permute-start.6 = (f32[4,16,10,1]{3,2,1,0:T(8,128)}, f32[4,16,10,1]{3,2,1,0:T(8,128)S(1)}, u32[]{:S(2)}, u32[]{:S(2)}) collective-permute-start(f32[4,16,10,1]{3,2,1,0:T(8,128)} %get-tuple-element.31), channel_id=1, source_target_pairs={{0,1},{1,2},{2,3},{3,0},{4,5},{5,6},{6,7},{7,4},{8,9},{9,10},{10,1... | collective-permute-start | bytes 7688 | tf_op jit(solution)/shard_map/ppermute | solution.py:16
  83.0 3.9 %collective-permute-start.7 = (f32[4,16,10,1]{3,2,1,0:T(8,128)S(1)}, f32[4,16,10,1]{3,2,1,0:T(8,128)S(1)}, u32[]{:S(2)}, u32[]{:S(2)}) collective-permute-start(f32[4,16,10,1]{3,2,1,0:T(8,128)S(1)} %get-tuple-element.32), channel_id=1, source_target_pairs={{1,0},{2,1},{3,2},{0,3},{5,4},{6,5},{7,6},{4,7},{9,8},{10,9},{11,1... | collective-permute-start | bytes 7688 | tf_op jit(solution)/shard_map/ppermute | solution.py:18
  87.1 5.7 %collective-permute-done.6 = f32[4,16,10,1]{3,2,1,0:T(8,128)S(1)} collective-permute-done((f32[4,16,10,1]{3,2,1,0:T(8,128)}, f32[4,16,10,1]{3,2,1,0:T(8,128)S(1)}, u32[]{:S(2)}, u32[]{:S(2)}) %collective-permute-start.6) | collective-permute-done | bytes 2592 | tf_op jit(solution)/shard_map/ppermute | solution.py:16
  92.8 6.9 %collective-permute-done.7 = f32[4,16,10,1]{3,2,1,0:T(8,128)S(1)} collective-permute-done((f32[4,16,10,1]{3,2,1,0:T(8,128)S(1)}, f32[4,16,10,1]{3,2,1,0:T(8,128)S(1)}, u32[]{:S(2)}, u32[]{:S(2)}) %collective-permute-start.7) | collective-permute-done | bytes 2592 | tf_op jit(solution)/shard_map/ppermute | solution.py:18
  99.7 0.7 broadcast_multiply_fusion.6
  101.3 1.9 %collective-permute-start.8 = (f32[4,16,1,128]{3,2,1,0:T(1,128)S(1)}, f32[4,16,1,128]{3,2,1,0:T(1,128)S(1)}, u32[]{:S(2)}, u32[]{:S(2)}) collective-permute-start(f32[4,16,1,128]{3,2,1,0:T(1,128)S(1)} %get-tuple-element.39), channel_id=1, source_target_pairs={{0,4},{4,8},{8,12},{12,16},{16,20},{20,24},{24,28},{28,32},{32,36}... | collective-permute-start | bytes 98312 | tf_op jit(solution)/shard_map/ppermute | solution.py:16
  103.3 12.5 %collective-permute-start.9 = (f32[4,16,1,128]{3,2,1,0:T(1,128)S(1)}, f32[4,16,1,128]{3,2,1,0:T(1,128)S(1)}, u32[]{:S(2)}, u32[]{:S(2)}) collective-permute-start(f32[4,16,1,128]{3,2,1,0:T(1,128)S(1)} %get-tuple-element.40), channel_id=1, source_target_pairs={{4,0},{8,4},{12,8},{16,12},{20,16},{24,20},{28,24},{32,28},{36,32}... | collective-permute-start | bytes 98312 | tf_op jit(solution)/shard_map/ppermute | solution.py:18
  115.8 1.6 collective-permute-done.9
  117.4 1.0 fusion.25
  118.4 3.1 %collective-permute-start.10 = (f32[4,16,10,1]{3,2,1,0:T(8,128)}, f32[4,16,10,1]{3,2,1,0:T(8,128)S(1)}, u32[]{:S(2)}, u32[]{:S(2)}) collective-permute-start(f32[4,16,10,1]{3,2,1,0:T(8,128)} %get-tuple-element.29), channel_id=1, source_target_pairs={{0,1},{1,2},{2,3},{3,0},{4,5},{5,6},{6,7},{7,4},{8,9},{9,10},{10,1... | collective-permute-start | bytes 7688 | tf_op jit(solution)/shard_map/ppermute | solution.py:16
  121.6 2.9 %collective-permute-start.11 = (f32[4,16,10,1]{3,2,1,0:T(8,128)S(1)}, f32[4,16,10,1]{3,2,1,0:T(8,128)S(1)}, u32[]{:S(2)}, u32[]{:S(2)}) collective-permute-start(f32[4,16,10,1]{3,2,1,0:T(8,128)S(1)} %get-tuple-element.30), channel_id=1, source_target_pairs={{1,0},{2,1},{3,2},{0,3},{5,4},{6,5},{7,6},{4,7},{9,8},{10,9},{11,1... | collective-permute-start | bytes 7688 | tf_op jit(solution)/shard_map/ppermute | solution.py:18
  124.7 5.0 %collective-permute-done.10 = f32[4,16,10,1]{3,2,1,0:T(8,128)S(1)} collective-permute-done((f32[4,16,10,1]{3,2,1,0:T(8,128)}, f32[4,16,10,1]{3,2,1,0:T(8,128)S(1)}, u32[]{:S(2)}, u32[]{:S(2)}) %collective-permute-start.10) | collective-permute-done | bytes 2592 | tf_op jit(solution)/shard_map/ppermute | solution.py:16
  129.7 8.0 %collective-permute-done.11 = f32[4,16,10,1]{3,2,1,0:T(8,128)S(1)} collective-permute-done((f32[4,16,10,1]{3,2,1,0:T(8,128)S(1)}, f32[4,16,10,1]{3,2,1,0:T(8,128)S(1)}, u32[]{:S(2)}, u32[]{:S(2)}) %collective-permute-start.11) | collective-permute-done | bytes 2592 | tf_op jit(solution)/shard_map/ppermute | solution.py:18
  137.8 0.7 broadcast_multiply_fusion.5
  139.4 1.9 %collective-permute-start.12 = (f32[4,16,1,128]{3,2,1,0:T(1,128)S(1)}, f32[4,16,1,128]{3,2,1,0:T(1,128)S(1)}, u32[]{:S(2)}, u32[]{:S(2)}) collective-permute-start(f32[4,16,1,128]{3,2,1,0:T(1,128)S(1)} %get-tuple-element.37), channel_id=1, source_target_pairs={{0,4},{4,8},{8,12},{12,16},{16,20},{20,24},{24,28},{28,32},{32,36}... | collective-permute-start | bytes 98312 | tf_op jit(solution)/shard_map/ppermute | solution.py:16
  141.3 12.8 %collective-permute-start.13 = (f32[4,16,1,128]{3,2,1,0:T(1,128)S(1)}, f32[4,16,1,128]{3,2,1,0:T(1,128)S(1)}, u32[]{:S(2)}, u32[]{:S(2)}) collective-permute-start(f32[4,16,1,128]{3,2,1,0:T(1,128)S(1)} %get-tuple-element.38), channel_id=1, source_target_pairs={{4,0},{8,4},{12,8},{16,12},{20,16},{24,20},{28,24},{32,28},{36,32}... | collective-permute-start | bytes 98312 | tf_op jit(solution)/shard_map/ppermute | solution.py:18
  154.2 1.6 collective-permute-done.13
  156.0 2.6 %collective-permute-start.14 = (f32[4,16,10,1]{3,2,1,0:T(8,128)S(1)}, f32[4,16,10,1]{3,2,1,0:T(8,128)S(1)}, u32[]{:S(2)}, u32[]{:S(2)}) collective-permute-start(f32[4,16,10,1]{3,2,1,0:T(8,128)S(1)} %get-tuple-element.27), channel_id=1, source_target_pairs={{0,1},{1,2},{2,3},{3,0},{4,5},{5,6},{6,7},{7,4},{8,9},{9,10},{10,1... | collective-permute-start | bytes 7688 | tf_op jit(solution)/shard_map/ppermute | solution.py:16
  158.6 3.3 %collective-permute-start.15 = (f32[4,16,10,1]{3,2,1,0:T(8,128)S(1)}, f32[4,16,10,1]{3,2,1,0:T(8,128)S(1)}, u32[]{:S(2)}, u32[]{:S(2)}) collective-permute-start(f32[4,16,10,1]{3,2,1,0:T(8,128)S(1)} %get-tuple-element.28), channel_id=1, source_target_pairs={{1,0},{2,1},{3,2},{0,3},{5,4},{6,5},{7,6},{4,7},{9,8},{10,9},{11,1... | collective-permute-start | bytes 7688 | tf_op jit(solution)/shard_map/ppermute | solution.py:18
  161.9 5.2 %collective-permute-done.14 = f32[4,16,10,1]{3,2,1,0:T(8,128)S(1)} collective-permute-done((f32[4,16,10,1]{3,2,1,0:T(8,128)S(1)}, f32[4,16,10,1]{3,2,1,0:T(8,128)S(1)}, u32[]{:S(2)}, u32[]{:S(2)}) %collective-permute-start.14) | collective-permute-done | bytes 2592 | tf_op jit(solution)/shard_map/ppermute | solution.py:16
  167.1 7.4 %collective-permute-done.15 = f32[4,16,10,1]{3,2,1,0:T(8,128)S(1)} collective-permute-done((f32[4,16,10,1]{3,2,1,0:T(8,128)S(1)}, f32[4,16,10,1]{3,2,1,0:T(8,128)S(1)}, u32[]{:S(2)}, u32[]{:S(2)}) %collective-permute-start.15) | collective-permute-done | bytes 2592 | tf_op jit(solution)/shard_map/ppermute | solution.py:18
  174.5 0.7 broadcast_multiply_fusion.4
  176.1 0.7 pad_maximum_fusion.5
  (60 shorter events, 7.1 us)
Async XLA Ops:
  0.0 16.7 %all-to-all-start = ((s32[4,1,64]{2,1,0:T(1,128)}), s32[4,1,64]{2,1,0:T(1,128)S(1)}, u32[]{:S(2)}, u32[]{:S(2)}) async-start(s32[4,1,64]{2,1,0:T(1,128)} %bitcast.39), calls=%async_computation | async-start | bytes 4096 | tf_op jit(solution)/shard_map/all_to_all | solution.py:71
  16.7 9.9 %all-to-all-start.1 = ((f32[4,64,128]{2,1,0:T(8,128)}), f32[4,64,128]{2,1,0:T(8,128)S(1)}, u32[]{:S(2)}, u32[]{:S(2)}) async-start(f32[4,64,128]{2,1,0:T(8,128)} %bitcast_multiply_fusion), calls=%async_computation.1 | async-start | bytes 262144 | tf_op jit(solution)/shard_map/all_to_all | solution.py:70
  28.1 1.8 %copy-start.6 = (f32[4,16,8,128]{3,2,1,0:T(8,128)S(1)}, f32[4,16,8,128]{3,2,1,0:T(8,128)}, u32[]{:S(2)}) copy-start(f32[4,16,8,128]{3,2,1,0:T(8,128)} %param.6) | copy-start | bytes 786436
  29.8 0.9 copy-start
  29.8 1.0 copy-start.4
  30.8 14.7 %collective-permute-start = (f32[10,16,1,128]{3,2,1,0:T(1,128)S(1)}, f32[10,16,1,128]{3,2,1,0:T(1,128)S(1)}, u32[]{:S(2)}, u32[]{:S(2)}) collective-permute-start(f32[10,16,1,128]{3,2,1,0:T(1,128)S(1)} %get-tuple-element.25), channel_id=1, source_target_pairs={{0,4},{4,8},{8,12},{12,16},{16,20},{20,24},{24,28},{28,32},{32,36}... | collective-permute-start | bytes 245768 | tf_op jit(solution)/shard_map/ppermute | solution.py:16
  32.8 13.8 %collective-permute-start.1 = (f32[10,16,1,128]{3,2,1,0:T(1,128)S(1)}, f32[10,16,1,128]{3,2,1,0:T(1,128)S(1)}, u32[]{:S(2)}, u32[]{:S(2)}) collective-permute-start(f32[10,16,1,128]{3,2,1,0:T(1,128)S(1)} %get-tuple-element.26), channel_id=1, source_target_pairs={{4,0},{8,4},{12,8},{16,12},{20,16},{24,20},{28,24},{32,28},{36,32}... | collective-permute-start | bytes 245768 | tf_op jit(solution)/shard_map/ppermute | solution.py:18
  46.6 2.0 %copy-start.5 = (f32[10,16,1,128]{3,2,1,0:T(1,128)}, f32[10,16,1,128]{3,2,1,0:T(1,128)S(1)}, u32[]{:S(2)}) copy-start(f32[10,16,1,128]{3,2,1,0:T(1,128)S(1)} %collective-permute-done.1) | copy-start | bytes 245764
  48.6 3.4 %copy-start.7 = (f32[10,16,10,1]{1,3,2,0:T(1,128)S(1)}, f32[10,16,10,1]{1,3,2,0:T(1,128)}, u32[]{:S(2)}) copy-start(f32[10,16,10,1]{1,3,2,0:T(1,128)} %copy.17) | copy-start | bytes 19204
  48.6 6.6 %copy-start.3 = (f32[32,1024]{0,1:T(8,128)S(1)}, f32[32,1024]{0,1:T(8,128)}, u32[]{:S(2)}) copy-start(f32[32,1024]{0,1:T(8,128)} %get-tuple-element.33) | copy-start | bytes 393220
  49.2 9.4 %collective-permute-start.3 = (f32[10,16,10,1]{1,3,2,0:T(1,128)S(1)}, f32[10,16,10,1]{1,3,2,0:T(1,128)S(1)}, u32[]{:S(2)}, u32[]{:S(2)}) collective-permute-start(f32[10,16,10,1]{1,3,2,0:T(1,128)S(1)} %copy.18), channel_id=1, source_target_pairs={{1,0},{2,1},{3,2},{0,3},{5,4},{6,5},{7,6},{4,7},{9,8},{10,9},{11,1... | collective-permute-start | bytes 19208 | tf_op jit(solution)/shard_map/ppermute | solution.py:18
  51.9 6.0 %collective-permute-start.2 = (f32[10,16,10,1]{1,3,2,0:T(1,128)S(1)}, f32[10,16,10,1]{1,3,2,0:T(1,128)S(1)}, u32[]{:S(2)}, u32[]{:S(2)}) collective-permute-start(f32[10,16,10,1]{1,3,2,0:T(1,128)S(1)} %copy-done.7), channel_id=1, source_target_pairs={{0,1},{1,2},{2,3},{3,0},{4,5},{5,6},{6,7},{7,4},{8,9},{9,10},{10,1... | collective-permute-start | bytes 19208 | tf_op jit(solution)/shard_map/ppermute | solution.py:16
  63.3 13.8 %collective-permute-start.4 = (f32[4,16,1,128]{3,2,1,0:T(1,128)S(1)}, f32[4,16,1,128]{3,2,1,0:T(1,128)S(1)}, u32[]{:S(2)}, u32[]{:S(2)}) collective-permute-start(f32[4,16,1,128]{3,2,1,0:T(1,128)S(1)} %get-tuple-element.41), channel_id=1, source_target_pairs={{0,4},{4,8},{8,12},{12,16},{16,20},{20,24},{24,28},{28,32},{32,36}... | collective-permute-start | bytes 98312 | tf_op jit(solution)/shard_map/ppermute | solution.py:16
  65.3 21.6 %copy-start.2 = (f32[32,1024]{0,1:T(8,128)S(1)}, f32[32,1024]{0,1:T(8,128)}, u32[]{:S(2)}) copy-start(f32[32,1024]{0,1:T(8,128)} %get-tuple-element.35) | copy-start | bytes 393220
  65.3 13.5 %collective-permute-start.5 = (f32[4,16,1,128]{3,2,1,0:T(1,128)S(1)}, f32[4,16,1,128]{3,2,1,0:T(1,128)S(1)}, u32[]{:S(2)}, u32[]{:S(2)}) collective-permute-start(f32[4,16,1,128]{3,2,1,0:T(1,128)S(1)} %get-tuple-element.42), channel_id=1, source_target_pairs={{4,0},{8,4},{12,8},{16,12},{20,16},{24,20},{28,24},{32,28},{36,32}... | collective-permute-start | bytes 98312 | tf_op jit(solution)/shard_map/ppermute | solution.py:18
  79.8 12.9 %collective-permute-start.6 = (f32[4,16,10,1]{3,2,1,0:T(8,128)}, f32[4,16,10,1]{3,2,1,0:T(8,128)S(1)}, u32[]{:S(2)}, u32[]{:S(2)}) collective-permute-start(f32[4,16,10,1]{3,2,1,0:T(8,128)} %get-tuple-element.31), channel_id=1, source_target_pairs={{0,1},{1,2},{2,3},{3,0},{4,5},{5,6},{6,7},{7,4},{8,9},{9,10},{10,1... | collective-permute-start | bytes 7688 | tf_op jit(solution)/shard_map/ppermute | solution.py:16
  83.0 16.7 %collective-permute-start.7 = (f32[4,16,10,1]{3,2,1,0:T(8,128)S(1)}, f32[4,16,10,1]{3,2,1,0:T(8,128)S(1)}, u32[]{:S(2)}, u32[]{:S(2)}) collective-permute-start(f32[4,16,10,1]{3,2,1,0:T(8,128)S(1)} %get-tuple-element.32), channel_id=1, source_target_pairs={{1,0},{2,1},{3,2},{0,3},{5,4},{6,5},{7,6},{4,7},{9,8},{10,9},{11,1... | collective-permute-start | bytes 7688 | tf_op jit(solution)/shard_map/ppermute | solution.py:18
  101.3 14.4 %collective-permute-start.8 = (f32[4,16,1,128]{3,2,1,0:T(1,128)S(1)}, f32[4,16,1,128]{3,2,1,0:T(1,128)S(1)}, u32[]{:S(2)}, u32[]{:S(2)}) collective-permute-start(f32[4,16,1,128]{3,2,1,0:T(1,128)S(1)} %get-tuple-element.39), channel_id=1, source_target_pairs={{0,4},{4,8},{8,12},{12,16},{16,20},{20,24},{24,28},{28,32},{32,36}... | collective-permute-start | bytes 98312 | tf_op jit(solution)/shard_map/ppermute | solution.py:16
  103.3 21.2 %copy-start.1 = (f32[32,1024]{0,1:T(8,128)S(1)}, f32[32,1024]{0,1:T(8,128)}, u32[]{:S(2)}) copy-start(f32[32,1024]{0,1:T(8,128)} %get-tuple-element.34) | copy-start | bytes 393220
  103.3 14.0 %collective-permute-start.9 = (f32[4,16,1,128]{3,2,1,0:T(1,128)S(1)}, f32[4,16,1,128]{3,2,1,0:T(1,128)S(1)}, u32[]{:S(2)}, u32[]{:S(2)}) collective-permute-start(f32[4,16,1,128]{3,2,1,0:T(1,128)S(1)} %get-tuple-element.40), channel_id=1, source_target_pairs={{4,0},{8,4},{12,8},{16,12},{20,16},{24,20},{28,24},{32,28},{36,32}... | collective-permute-start | bytes 98312 | tf_op jit(solution)/shard_map/ppermute | solution.py:18
  118.4 11.3 %collective-permute-start.10 = (f32[4,16,10,1]{3,2,1,0:T(8,128)}, f32[4,16,10,1]{3,2,1,0:T(8,128)S(1)}, u32[]{:S(2)}, u32[]{:S(2)}) collective-permute-start(f32[4,16,10,1]{3,2,1,0:T(8,128)} %get-tuple-element.29), channel_id=1, source_target_pairs={{0,1},{1,2},{2,3},{3,0},{4,5},{5,6},{6,7},{7,4},{8,9},{9,10},{10,1... | collective-permute-start | bytes 7688 | tf_op jit(solution)/shard_map/ppermute | solution.py:16
  121.6 16.2 %collective-permute-start.11 = (f32[4,16,10,1]{3,2,1,0:T(8,128)S(1)}, f32[4,16,10,1]{3,2,1,0:T(8,128)S(1)}, u32[]{:S(2)}, u32[]{:S(2)}) collective-permute-start(f32[4,16,10,1]{3,2,1,0:T(8,128)S(1)} %get-tuple-element.30), channel_id=1, source_target_pairs={{1,0},{2,1},{3,2},{0,3},{5,4},{6,5},{7,6},{4,7},{9,8},{10,9},{11,1... | collective-permute-start | bytes 7688 | tf_op jit(solution)/shard_map/ppermute | solution.py:18
  139.4 14.8 %collective-permute-start.12 = (f32[4,16,1,128]{3,2,1,0:T(1,128)S(1)}, f32[4,16,1,128]{3,2,1,0:T(1,128)S(1)}, u32[]{:S(2)}, u32[]{:S(2)}) collective-permute-start(f32[4,16,1,128]{3,2,1,0:T(1,128)S(1)} %get-tuple-element.37), channel_id=1, source_target_pairs={{0,4},{4,8},{8,12},{12,16},{16,20},{20,24},{24,28},{28,32},{32,36}... | collective-permute-start | bytes 98312 | tf_op jit(solution)/shard_map/ppermute | solution.py:16
  141.3 14.4 %collective-permute-start.13 = (f32[4,16,1,128]{3,2,1,0:T(1,128)S(1)}, f32[4,16,1,128]{3,2,1,0:T(1,128)S(1)}, u32[]{:S(2)}, u32[]{:S(2)}) collective-permute-start(f32[4,16,1,128]{3,2,1,0:T(1,128)S(1)} %get-tuple-element.38), channel_id=1, source_target_pairs={{4,0},{8,4},{12,8},{16,12},{20,16},{24,20},{28,24},{32,28},{36,32}... | collective-permute-start | bytes 98312 | tf_op jit(solution)/shard_map/ppermute | solution.py:18
  156.0 11.1 %collective-permute-start.14 = (f32[4,16,10,1]{3,2,1,0:T(8,128)S(1)}, f32[4,16,10,1]{3,2,1,0:T(8,128)S(1)}, u32[]{:S(2)}, u32[]{:S(2)}) collective-permute-start(f32[4,16,10,1]{3,2,1,0:T(8,128)S(1)} %get-tuple-element.27), channel_id=1, source_target_pairs={{0,1},{1,2},{2,3},{3,0},{4,5},{5,6},{6,7},{7,4},{8,9},{9,10},{10,1... | collective-permute-start | bytes 7688 | tf_op jit(solution)/shard_map/ppermute | solution.py:16
  158.6 15.9 %collective-permute-start.15 = (f32[4,16,10,1]{3,2,1,0:T(8,128)S(1)}, f32[4,16,10,1]{3,2,1,0:T(8,128)S(1)}, u32[]{:S(2)}, u32[]{:S(2)}) collective-permute-start(f32[4,16,10,1]{3,2,1,0:T(8,128)S(1)} %get-tuple-element.28), channel_id=1, source_target_pairs={{1,0},{2,1},{3,2},{0,3},{5,4},{6,5},{7,6},{4,7},{9,8},{10,9},{11,1... | collective-permute-start | bytes 7688 | tf_op jit(solution)/shard_map/ppermute | solution.py:18
where the time goes:
time: 178 us; the launch traced here: 177 us
  starting transfers between devices  98.8 us (56%)
  waiting for transfers between devices  53.1 us (30%)
  other arithmetic  14.5 us (8%)
  local copies, waits for them, and re-layouts  9.9 us (6%)
    ppermute x8, starting transfers between devices, with_halo(): lax.ppermute(head, axis, [((i + 1) % count, i) for i in range(count)])  61.7 us
    ppermute x8, waiting for transfers between devices, with_halo(): lax.ppermute(head, axis, [((i + 1) % count, i) for i in range(count)])  28.1 us
    ppermute x8, starting transfers between devices, with_halo(): lax.ppermute(tail, axis, [(i, (i + 1) % count) for i in range(count)])  19.7 us
    ppermute x8, waiting for transfers between devices, with_halo(): lax.ppermute(tail, axis, [(i, (i + 1) % count) for i in range(count)])  19.5 us
    all_to_all x1, starting transfers between devices, body(): lax.all_to_all(obs_column[0], 'lon', split_axis=0, concat_axis=0, tiled=T...  12.6 us
    all_to_all x1, starting transfers between devices, body(): lax.all_to_all(outgoing, 'lon', split_axis=0, concat_axis=0, tiled=True)  4.74 us
    slice x5, local copies, waits for them, and re-layouts, with_halo(): lax.slice_in_dim(cells, cells.shape[dim] - width, cells.shape[dim], axis=...  3.96 us
    all_to_all x1, waiting for transfers between devices, body(): lax.all_to_all(outgoing, 'lon', split_axis=0, concat_axis=0, tiled=True)  3.89 us
  transfers between devices with their start and end apart: 18, of which 14 were waited for; matrix products, arithmetic and copies ran while one was open for 3% of the time, Pallas kernels for 0%

commit v1 on v0

v1 whole, which is shorter than its diff:
```python
import functools

import jax
import jax.numpy as jnp
from jax import lax
from jax.experimental import pallas as pl
from jax.experimental.pallas import tpu as pltpu
from jax.sharding import PartitionSpec as P

DIFFUSION = 0.1
F32 = jnp.float32
BF16 = jnp.bfloat16

TARGET_ROW = 64
EDGE_ROW = 72
STRIP_ROW = 136
LON_ROWS = 216

A_AT, B_AT, C_AT, STRIP_AT = 16, 18, 19, 23
LAT_ROWS = 25 * 16
CENTRE = 1.0 - 4.0 * DIFFUSION


def pieces(values):
    high = values.astype(BF16)
    rest = values - high.astype(F32)
    middle = rest.astype(BF16)
    low = (rest - middle.astype(F32)).astype(BF16)
    return high, middle, low


def lanes_of(rows):
    return lax.broadcasted_iota(jnp.int32, (rows, 128), 1)


def levels(ref, field, row, first=0, count=16):
    return ref[field, pl.ds(first * 8 + row, count, stride=8), :]


def pack_kernel(*refs):
    sources, out_ref, copies_of, sems = refs[:6], refs[6], refs[7:13], refs[13]
    copies = [pltpu.make_async_copy(sources[i], copies_of[i], sems.at[i]) for i in range(6)]
    for copy in copies:
        copy.start()
    for copy in copies[:3]:
        copy.wait()
    count_ref, column_ref, values_ref, lam_ref, winds_ref, coupling_ref = copies_of
    slot = lax.broadcasted_iota(jnp.int32, (64, 128), 0)
    blocks = []
    columns = []
    for tile in range(4):
        block = jnp.where(slot < count_ref[0, tile], values_ref[tile], 0.0)
        blocks.append(block)
        column = column_ref[tile : tile + 1, :]
        columns.append(column)
        out_ref[tile, 0:64, :] = block
        wide = jnp.concatenate([column, jnp.zeros((1, 64), jnp.int32)], axis=1)
        out_ref[tile, TARGET_ROW:EDGE_ROW, :] = jnp.broadcast_to(wide.astype(F32), (8, 128))

    cell = lax.broadcasted_iota(jnp.int32, (64, 128), 0)
    side = cell & 7
    wanted = (cell >> 3) * 128 + jnp.where(side < 4, 124 + side, side - 4)
    allowed = (lanes_of(64) < 64) == (side < 4)
    for tile in range(4):
        left, right = (tile + 3) % 4, (tile + 1) % 4
        target = jnp.concatenate([columns[left], columns[right]], axis=1)
        hit = jnp.where(jnp.logical_and(jnp.broadcast_to(target, (64, 128)) == wanted, allowed), 1.0, 0.0)
        hit = hit.astype(BF16)
        both = jnp.concatenate([blocks[left], blocks[right]], axis=0)
        total = jnp.zeros((64, 128), F32)
        for piece in pieces(both):
            total = total + jnp.dot(hit, piece, preferred_element_type=F32)
        out_ref[tile, EDGE_ROW:STRIP_ROW, :] = total

    for copy in copies[3:]:
        copy.wait()
    lane = lanes_of(8)
    row = STRIP_ROW
    for ref, fields in ((lam_ref, 4), (winds_ref, 2), (coupling_ref, 4)):
        for field in range(fields):
            strip = jnp.zeros((8, 128), F32)
            for half in range(2):
                for r in range(8):
                    at = half * 64 + r * 8
                    moved = pltpu.roll(levels(ref, field, r, half * 8, 8), (at + 4) % 128, 1)
                    strip = jnp.where(jnp.logical_and(lane >= at, lane < at + 8), moved, strip)
            for tile in range(4):
                out_ref[tile, row : row + 8, :] = strip
            row += 8


def strip_lane(plane, way):
    return ((plane % 16) * 8 + way * (88 if plane == A_AT + 1 else 72)) % 128


def once(make):
    made = {}

    def get(*key):
        if key not in made:
            made[key] = make(*key)
        return made[key]

    return get


def along(x, to_left, to_right, beside, at, lane):
    p_right, p_left = to_left * x, to_right * x
    edge = pltpu.roll(beside, (128 - (at + 4)) % 128, 1)
    right = jnp.where(lane == 127, edge, pltpu.roll(p_right, 127, 1))
    left = jnp.where(lane == 0, edge, pltpu.roll(p_left, 1, 1))
    return right + left, jnp.where(lane == 0, p_right, p_left)


def insert(inner, pair, at, lane):
    moved = pltpu.roll(pair, (at + 4) % 128, 1)
    return jnp.where(jnp.logical_or(lane == at + 4, lane == at + 3), moved, inner)


def strip_along(rolled_right, rolled_left, inner, side):
    right = jnp.where(side == 3, pltpu.roll(inner, 127, 1), rolled_right)
    left = jnp.where(side == 4, pltpu.roll(inner, 1, 1), rolled_left)
    return right + left


def own_steps(lam_ref, winds_ref, coupling_ref, force_ref, strips_ref, wanted, keep):
    lane = lanes_of(8)
    side = lane & 7
    strip_row = (lane >> 3) & 7

    def force(row, instant, field, half):
        at = instant * 32 + field * 16 + half * 8
        return force_ref[row, at : at + 8, :]

    half_wind = once(lambda axis, row, half: 0.5 * levels(winds_ref, axis, row, half * 8, 8))
    up_weight = once(lambda row, half: DIFFUSION + half_wind(0, row, half))
    down_weight = once(lambda row, half: DIFFUSION - half_wind(0, row, half))
    right_weight = once(lambda row, half: DIFFUSION + half_wind(1, row, half))
    left_weight = once(lambda row, half: DIFFUSION - half_wind(1, row, half))

    def strip(place):
        return strips_ref[place * 8 : place * 8 + 8, :]

    half_a, half_b = 0.5 * strip(4), 0.5 * strip(5)
    strip_up, strip_down = DIFFUSION + half_a, DIFFUSION - half_a
    strip_right, strip_left = DIFFUSION + half_b, DIFFUSION - half_b

    u = [{}, {}, {}, {}]
    for field in range(4):
        for half in range(2):
            for row in range(8):
                value = levels(lam_ref, field, row, half * 8, 8)
                if field >= 2:
                    value = value + force(row, 3, field - 2, half)
                u[field][row, half] = value
    strips = [strip(field) for field in range(4)]
    keep(0, u, strips)
    for step, rows in enumerate(wanted, 1):
        last = step == 4
        later = [{}, {}, {}, {}]
        later_strips = []
        for field in range(4):
            x = u[field]
            rolled_right = pltpu.roll(strip_right * strips[field], 127, 1)
            rolled_left = pltpu.roll(strip_left * strips[field], 1, 1)
            beside = jnp.where(side == 3, rolled_right, rolled_left)
            inner = beside
            for half in range(2):
                for row in rows:
                    at = half * 64 + row * 8
                    shares, pair = along(
                        x[row, half], right_weight(row, half), left_weight(row, half), beside, at, lane
                    )
                    total = CENTRE * x[row, half] + shares
                    if row < 7:
                        total = total + up_weight(row + 1, half) * x[row + 1, half]
                    if row > 0:
                        total = total + down_weight(row - 1, half) * x[row - 1, half]
                    if field < 2:
                        first = levels(coupling_ref, field, row, half * 8, 8)
                        second = levels(coupling_ref, field + 2, row, half * 8, 8)
                        total = total - (first * u[2][row, half] + second * u[3][row, half])
                    elif not last:
                        total = total + force(row, 3 - step, field - 2, half)
                    later[field][row, half] = total
                    if not last:
                        inner = insert(inner, pair, at, lane)
            if not last:
                total = CENTRE * strips[field] + strip_along(rolled_right, rolled_left, inner, side)
                total = total + jnp.where(strip_row == 7, 0.0, pltpu.roll(strip_up * strips[field], 120, 1))
                total = total + jnp.where(strip_row == 0, 0.0, pltpu.roll(strip_down * strips[field], 8, 1))
                if field < 2:
                    total = total - (strip(6 + field) * strips[2] + strip(8 + field) * strips[3])
                else:
                    total = total + strip(10 + 2 * (step - 1) + field - 2)
                later_strips.append(total)
        u, strips = later, later_strips
        keep(step, u, strips)


def halo_kernel(place_ref, got_ref, lam_ref, winds_ref, coupling_ref, even_ref, odd_ref, force_ref, strips_ref):
    is_even = lax.rem(place_ref[0], 2) == 0
    tile = place_ref[1]
    lane = lanes_of(8)
    lane1 = lanes_of(1)

    rows = [got_ref[s, TARGET_ROW : TARGET_ROW + 1, :] for s in range(4)]
    halves = [jnp.where(lane1 < 64, rows[s], pltpu.roll(rows[s + 1], 64, 1)) for s in (0, 2)]
    target = jnp.concatenate(halves, axis=1).astype(jnp.int32)
    blocks = jnp.concatenate([got_ref[s, 0:64, :] for s in range(4)], axis=0)
    stacked = jnp.concatenate(pieces(blocks.T), axis=0)
    cell = lax.broadcasted_iota(jnp.int32, (256, 256), 0)
    for pair in range(4):
        hit = jnp.where(jnp.broadcast_to(target, (256, 256)) == cell + pair * 256, 1.0, 0.0).astype(BF16)
        three = lax.dot_general(stacked, hit, (((1,), (1,)), ((), ())), preferred_element_type=F32)
        both = three[0:128] + three[128:256] + three[256:384]
        force_ref[2 * pair] = both[:, 0:128]
        force_ref[2 * pair + 1] = both[:, 128:256]

    edge = got_ref[0, EDGE_ROW:STRIP_ROW, :]
    for s in range(1, 4):
        edge = edge + got_ref[s, EDGE_ROW:STRIP_ROW, :]
    edge = jnp.concatenate([edge, edge], axis=0).T

    def edge_strip(instant, field):
        at = instant * 32 + field * 16
        return jnp.where(lane < 64, edge[at : at + 8], edge[at + 8 : at + 16])

    left = lax.rem(tile + 3, 4)
    right = lax.rem(tile + 1, 4)
    for field in range(10):
        at = STRIP_ROW + field * 8
        strip = jnp.where((lane & 7) < 4, got_ref[left, at : at + 8, :], got_ref[right, at : at + 8, :])
        if field in (2, 3):
            strip = strip + edge_strip(3, field - 2)
        strips_ref[field * 8 : field * 8 + 8, :] = strip
    for place, (instant, field) in enumerate(((2, 0), (2, 1), (1, 0), (1, 1), (0, 0), (0, 1))):
        strips_ref[80 + place * 8 : 88 + place * 8, :] = edge_strip(instant, field)

    sides = {}

    def put(plane, half, up, down):
        at = plane * 16 + half * 8
        even_ref[at : at + 8, :] = jnp.where(is_even, up, down)
        odd_ref[at : at + 8, :] = jnp.where(is_even, down, up)

    def put_strip(plane, packed, up_row, down_row):
        for half in range(2):
            for way, row in ((0, up_row), (1, down_row)):
                at = strip_lane(plane, way)
                mine = jnp.logical_and(lane >= at, lane < at + 8)
                key = (STRIP_AT + plane // 16, half, way)
                moved = pltpu.roll(packed, (at - half * 64 - row * 8) % 128, 1)
                sides[key] = jnp.where(mine, moved, sides.get(key, 0.0))

    def keep(step, u, strips):
        for field in range(4):
            plane = step * 4 + field
            for half in range(2):
                put(plane, half, u[field][7, half], u[field][0, half])
            if step < 3:
                put_strip(plane, strips[field], 7, 0)

    own_steps(
        lam_ref,
        winds_ref,
        coupling_ref,
        force_ref,
        strips_ref,
        ((0, 1, 2, 5, 6, 7), (0, 1, 6, 7), (0, 7)),
        keep,
    )
    for plane, ref, field, depth in (
        (A_AT, winds_ref, 0, 0),
        (A_AT + 1, winds_ref, 0, 1),
        (B_AT, winds_ref, 1, 0),
        (C_AT, coupling_ref, 0, 0),
        (C_AT + 1, coupling_ref, 1, 0),
        (C_AT + 2, coupling_ref, 2, 0),
        (C_AT + 3, coupling_ref, 3, 0),
    ):
        for half in range(2):
            put(plane, half, levels(ref, field, 7 - depth, half * 8, 8), levels(ref, field, depth, half * 8, 8))
        place = field + (4 if ref is winds_ref else 6)
        put_strip(plane, strips_ref[place * 8 : place * 8 + 8, :], 7 - depth, depth)
    for plane in (STRIP_AT, STRIP_AT + 1):
        for half in range(2):
            put(plane, half, sides[plane, half, 0], sides[plane, half, 1])


def own_kernel(force_ref, strips_ref, lam_ref, winds_ref, coupling_ref, out_ref, wide_ref):
    every = tuple(range(8))

    def widen(place, packed):
        for half in range(2):
            at = (place * 2 + half) * 8
            wide_ref[at : at + 8, :] = pltpu.roll(packed, 16 if half == 0 else 80, 1)

    def keep(step, u, strips):
        for field in range(4):
            if step < 3:
                widen(step * 4 + field, strips[field])
            if step == 4:
                for half in range(2):
                    for row in range(8):
                        out_ref[field, row, half * 8 : half * 8 + 8, :] = u[field][row, half]

    for place in range(6):
        widen(12 + place, strips_ref[32 + place * 8 : 40 + place * 8, :])
    own_steps(lam_ref, winds_ref, coupling_ref, force_ref, strips_ref, (every,) * 4, keep)


def join_kernel(
    place_ref,
    odd_ref,
    even_ref,
    sent_odd_ref,
    sent_even_ref,
    own_ref,
    wide_ref,
    winds_ref,
    coupling_ref,
    out_ref,
    border_ref,
):
    band = place_ref[0]
    is_even = lax.rem(band, 2) == 0
    low_mask = jnp.where(band > 0, 1.0, 0.0).astype(F32)
    high_mask = jnp.where(band < place_ref[2] - 1, 1.0, 0.0).astype(F32)
    lane = lanes_of(8)
    side = lane & 7
    strip_row = (lane >> 3) - 2
    strip_mask = jnp.where(strip_row < 0, low_mask, jnp.where(strip_row > 7, high_mask, 1.0))

    def chosen(first, second):
        def get(plane, half):
            at = plane * 16 + half * 8
            return jnp.where(is_even, first[at : at + 8, :], second[at : at + 8, :])

        return once(get)

    low, high = chosen(odd_ref, even_ref), chosen(even_ref, odd_ref)
    up, down = chosen(sent_even_ref, sent_odd_ref), chosen(sent_odd_ref, sent_even_ref)
    border_of = {-1: low, 0: down, 7: up, 8: high}

    def outer(first, row, half, own):
        if row < 0:
            return low(first - 1 - row, half)
        if row > 7:
            return high(first + row - 8, half)
        return own

    def half_wind(axis, row, half):
        own = levels(winds_ref, axis, row, half * 8, 8) if 0 <= row <= 7 else None
        return 0.5 * outer(A_AT if axis == 0 else B_AT, row, half, own)

    half_wind = once(half_wind)
    up_weight = once(lambda row, half: DIFFUSION + half_wind(0, row, half))
    down_weight = once(lambda row, half: DIFFUSION - half_wind(0, row, half))
    right_weight = once(lambda row, half: DIFFUSION + half_wind(1, row, half))
    left_weight = once(lambda row, half: DIFFUSION - half_wind(1, row, half))

    def couple(field, row, half):
        own = levels(coupling_ref, field, row, half * 8, 8) if 0 <= row <= 7 else None
        return outer(C_AT + field, row, half, own)

    couple = once(couple)

    def met(plane, half):
        at = strip_lane(plane, 0)
        mine = jnp.logical_and(lane >= at, lane < at + 8)
        both = jnp.where(mine, low(STRIP_AT + plane // 16, half), high(STRIP_AT + plane // 16, half))
        return pltpu.roll(both, ((0 if plane == A_AT + 1 else 8) - at) % 128, 1)

    inside = jnp.logical_and(strip_row >= 0, strip_row <= 7)

    def strip(place, plane, half):
        at = (place * 2 + half) * 8
        return jnp.where(inside, wide_ref[at : at + 8, :], met(plane, half))

    for plane in range(12):
        for half in range(2):
            at = (plane * 2 + half) * 8
            border_ref[at : at + 8, :] = strip(plane, plane, half)
    deepest = jnp.logical_or(strip_row == -2, strip_row == 9)
    strip_a = [
        0.5 * jnp.where(deepest, met(A_AT + 1, half), strip(12, A_AT, half)) for half in range(2)
    ]
    strip_b = [0.5 * strip(13, B_AT, half) for half in range(2)]
    strip_c = [[strip(14 + field, C_AT + field, half) for half in range(2)] for field in range(4)]

    e = [{}, {}, {}, {}]
    strips = [[None, None] for _ in range(4)]
    reach = ((-1, 0), (-2, -1, 0, 1), (-1, 0, 1, 2), (0, 1, 2, 3))
    for step in range(4):
        last = step == 3
        rows = reach[step] + tuple(7 - row for row in reach[step])
        later = [{}, {}, {}, {}]
        later_strips = [[None, None] for _ in range(4)]
        for field in range(4):
            x = e[field]
            plane = step * 4 + field
            for half in range(2):
                xs = strips[field][half]
                if step > 0:
                    rolled_right = pltpu.roll((DIFFUSION + strip_b[half]) * xs, 127, 1)
                    rolled_left = pltpu.roll((DIFFUSION - strip_b[half]) * xs, 1, 1)
                    beside = jnp.where(side == 3, rolled_right, rolled_left)
                    inner = beside
                for row in rows:
                    terms = []
                    if (row, half) in x:
                        here = x[row, half]
                        at = (row + 2) * 8
                        shares, pair = along(
                            here, right_weight(row, half), left_weight(row, half), beside, at, lane
                        )
                        local = CENTRE * here + shares
                        if field < 2:
                            local = local - (
                                couple(field, row, half) * e[2][row, half]
                                + couple(field + 2, row, half) * e[3][row, half]
                            )
                        terms.append(local)
                        if not last:
                            inner = insert(inner, pair, at, lane)
                    for near, crossing, weight in (
                        (row + 1, (0, 8), up_weight),
                        (row - 1, (-1, 7), down_weight),
                    ):
                        parts = []
                        if (near, half) in x:
                            parts.append(x[near, half])
                        if near in crossing:
                            parts.append(border_of[near](plane, half))
                        if parts:
                            terms.append(weight(near, half) * sum(parts[1:], parts[0]))
                    total = sum(terms[1:], terms[0])
                    if row == -1:
                        total = total * low_mask
                    if row == 8:
                        total = total * high_mask
                    if last:
                        total = total + own_ref[field, row, half * 8 : half * 8 + 8, :]
                        out_ref[field, pl.ds(half * 64 + row, 8, stride=8), :] = total
                    else:
                        later[field][row, half] = total
                if not last:
                    at = (plane * 2 + half) * 8
                    border = border_ref[at : at + 8, :]
                    from_above = jnp.where(jnp.logical_or(strip_row == 0, strip_row == 8), border, 0.0)
                    from_below = jnp.where(jnp.logical_or(strip_row == -1, strip_row == 7), border, 0.0)
                    if step > 0:
                        from_above, from_below = from_above + xs, from_below + xs
                    total = pltpu.roll((DIFFUSION + strip_a[half]) * from_above, 120, 1)
                    total = total + pltpu.roll((DIFFUSION - strip_a[half]) * from_below, 8, 1)
                    if step > 0:
                        total = total + CENTRE * xs + strip_along(rolled_right, rolled_left, inner, side)
                        if field < 2:
                            total = total - (
                                strip_c[field][half] * strips[2][half] + strip_c[field + 2][half] * strips[3][half]
                            )
                    later_strips[field][half] = total * strip_mask
        e, strips = later, later_strips


def vmem(count):
    return [pl.BlockSpec(memory_space=pltpu.VMEM)] * count


SMEM = pl.BlockSpec(memory_space=pltpu.SMEM)


def params(mebibytes=24):
    return pltpu.CompilerParams(vmem_limit_bytes=mebibytes * 1024 * 1024)


def body(lam_end, winds, coupling, obs_values, obs_column, obs_count):
    bands = lax.axis_size("lat")
    tiles = lax.axis_size("lon")
    lam = lam_end.reshape(4, 128, 128)
    wind = winds.reshape(2, 128, 128)
    couple = coupling.reshape(4, 128, 128)
    place = jnp.stack([lax.axis_index("lat"), lax.axis_index("lon"), jnp.int32(bands)]).astype(jnp.int32)

    message = pl.pallas_call(
        pack_kernel,
        out_shape=jax.ShapeDtypeStruct((tiles, LON_ROWS, 128), F32),
        in_specs=[pl.BlockSpec(memory_space=pltpu.HBM)] * 6,
        out_specs=vmem(1)[0],
        scratch_shapes=[
            pltpu.SMEM((1, 4), jnp.int32),
            pltpu.VMEM((4, 64), jnp.int32),
            pltpu.VMEM((4, 64, 128), F32),
            pltpu.VMEM((4, 128, 128), F32),
            pltpu.VMEM((2, 128, 128), F32),
            pltpu.VMEM((4, 128, 128), F32),
            pltpu.SemaphoreType.DMA((6,)),
        ],
        compiler_params=params(60),
        name="pack_blocks_and_strips",
    )(obs_count, obs_column[0], obs_values[0], lam, wind, couple)
    got = lax.all_to_all(message, "lon", split_axis=0, concat_axis=0, tiled=True)

    halo = jax.ShapeDtypeStruct((LAT_ROWS, 128), F32)
    even, odd, force, strips = pl.pallas_call(
        halo_kernel,
        out_shape=(
            halo,
            halo,
            jax.ShapeDtypeStruct((8, 128, 128), F32),
            jax.ShapeDtypeStruct((128, 128), F32),
        ),
        in_specs=[SMEM] + vmem(4),
        out_specs=tuple(vmem(4)),
        compiler_params=params(),
        name="scatter_and_halo",
    )(place, got, lam, wind, couple)
    swap = lambda first: [p for i in range(first, bands - 1, 2) for p in ((i, i + 1), (i + 1, i))]
    got_odd = lax.ppermute(odd, "lat", swap(1))
    got_even = lax.ppermute(even, "lat", swap(0))

    own, wide = pl.pallas_call(
        own_kernel,
        out_shape=(jax.ShapeDtypeStruct((4, 8, 16, 128), F32), jax.ShapeDtypeStruct((288, 128), F32)),
        in_specs=vmem(5),
        out_specs=tuple(vmem(2)),
        compiler_params=params(),
        cost_estimate=pl.CostEstimate(flops=10_000_000, bytes_accessed=2_000_000, transcendentals=0),
        name="own_steps",
    )(force, strips, lam, wind, couple)

    out = pl.pallas_call(
        join_kernel,
        out_shape=jax.ShapeDtypeStruct((4, 128, 128), F32),
        in_specs=[SMEM] + vmem(8),
        out_specs=vmem(1)[0],
        scratch_shapes=[pltpu.VMEM((192, 128), F32)],
        compiler_params=params(),
        name="join_bands",
    )(place, got_odd, got_even, odd, even, own, wide, wind, couple)
    return out.reshape(lam_end.shape)


def solution(mesh):
    return jax.shard_map(
        body,
        mesh=mesh,
        in_specs=(
            P(None, None, "lat", "lon"),
            P(None, None, "lat", "lon"),
            P(None, None, "lat", "lon"),
            P(("lat", "lon"), None, None, None),
            P(("lat", "lon"), None, None),
            P(("lat", "lon"), None),
        ),
        out_specs=P(None, None, "lat", "lon"),
        check_vma=False,
    )
```

time: 178 us -> 41.6 us (0.23)
  the two profiles are of different devices: /device:TPU:8 before, /device:TPU:512 now
where the time goes in v1:
time: 41.6 us; the launch traced here: 41.4 us
  waiting for transfers between devices  16.3 us (39%)
  starting transfers between devices  15.6 us (38%)
  Pallas kernels  9.3 us (22%)
    all_to_all x1, waiting for transfers between devices, body(): lax.all_to_all(message, 'lon', split_axis=0, concat_axis=0, tiled=True)  12.7 us
    ppermute x1, starting transfers between devices, body(): got_odd = lax.ppermute(odd, 'lat', swap(1))  8.67 us
    all_to_all x1, starting transfers between devices, body(): lax.all_to_all(message, 'lon', split_axis=0, concat_axis=0, tiled=True)  5.01 us
    ppermute x1, waiting for transfers between devices, body(): got_odd = lax.ppermute(odd, 'lat', swap(1))  3.66 us
    pallas_call x1, Pallas kernels, body(): pl.pallas_call(join_kernel, out_shape=jax.ShapeDtypeStruct((4, 128, 128),...  2.83 us
    pallas_call x1, Pallas kernels, body(): pl.pallas_call(own_kernel, out_shape=(jax.ShapeDtypeStruct((4, 8, 16, 128...  2.4 us
    pallas_call x1, Pallas kernels, body(): pl.pallas_call(pack_kernel, out_shape=jax.ShapeDtypeStruct((tiles, LON_RO...  2.26 us
    ppermute x1, starting transfers between devices, body(): got_even = lax.ppermute(even, 'lat', swap(0))  1.92 us
  transfers between devices with their start and end apart: 3, of which 2 were waited for; matrix products, arithmetic and copies ran while one was open for 0% of the time, Pallas kernels for 6%

profile of v1, /device:TPU:512, one launch (start us, length us, event | category | flops | bytes accessed | tf_op | source)
XLA Modules:
  0.0 41.4 jit_solution(3378308652882162488)
XLA Ops:
  0.0 2.3 %pack_blocks_and_strips.1 = f32[4,216,128]{2,1,0:T(8,128)} custom-call(s32[1,4]{1,0:T(1,128)} %refs_0_.1, s32[4,64]{1,0:T(4,128)} %bitcast.20, f32[4,64,128]{2,1,0:T(8,128)} %bitcast.19, f32[4,128,128]{2,1,0:T(8,128)} %bitcast.12, f32[2,128,128]{2,1,0:T(8,128)} %bitcast.15, f32[4,128,128]{2,1,0:T(8,128)} %bitcast.8), custom_call_target="tpu_custom_call" | custom-call | tf_op jit(solution)/shard_map/pack_blocks_and_strips/pallas_call | solution.py:486
  2.3 0.0 copy-start
  2.3 0.0 copy-start.1
  2.3 0.0 copy-start.2
  2.3 5.0 %all-to-all-start = ((f32[4,216,128]{2,1,0:T(8,128)}), f32[4,216,128]{2,1,0:T(8,128)S(1)}, u32[]{:S(2)}, u32[]{:S(2)}) async-start(f32[4,216,128]{2,1,0:T(8,128)} %pack_blocks_and_strips.1), calls=%async_computation | async-start | bytes 884736 | tf_op jit(solution)/shard_map/all_to_all | solution.py:503
  7.3 0.1 pad_add_fusion.place_ref
  7.4 12.7 %all-to-all-done.got_ref = f32[4,216,128]{2,1,0:T(8,128)S(1)} async-done(((f32[4,216,128]{2,1,0:T(8,128)}), f32[4,216,128]{2,1,0:T(8,128)S(1)}, u32[]{:S(2)}, u32[]{:S(2)}) %all-to-all-start) | async-done | bytes 442400 | tf_op jit(solution)/shard_map/all_to_all | solution.py:503
  20.1 0.0 copy-done
  20.1 0.0 copy-done.1
  20.1 0.0 copy-done.2
  20.1 1.8 %scatter_and_halo.1 = (f32[400,128]{1,0:T(8,128)S(1)}, f32[400,128]{1,0:T(8,128)S(1)}, f32[8,128,128]{2,1,0:T(8,128)S(1)}, f32[128,128]{1,0:T(8,128)S(1)}) custom-call(s32[3]{0:T(128)S(1)} %pad_add_fusion.place_ref, f32[4,216,128]{2,1,0:T(8,128)S(1)} %all-to-all-done.got_ref, f32[4,128,128]{2,1,0:T(8,128)S(1)} %bitcast.13, f32[2,128,128]{2,1,0:T(8,128)S(1)} %bitcast.16, ...), custom_call_target="tpu_custom_call" | custom-call | tf_op jit(solution)/shard_map/scatter_and_halo/pallas_call | solution.py:506
  21.9 8.7 %collective-permute-start = (f32[400,128]{1,0:T(8,128)S(1)}, f32[400,128]{1,0:T(8,128)S(1)}, u32[]{:S(2)}, u32[]{:S(2)}) collective-permute-start(f32[400,128]{1,0:T(8,128)S(1)} %get-tuple-element.11.sent_odd_ref), channel_id=1, source_target_pairs={{4,8},{8,4},{12,16},{16,12},{20,24},{24,20},{28,32},{32,28},{36,40... | collective-permute-start | bytes 614408 | tf_op jit(solution)/shard_map/ppermute | solution.py:520
  30.6 1.9 %collective-permute-start.1 = (f32[400,128]{1,0:T(8,128)S(1)}, f32[400,128]{1,0:T(8,128)S(1)}, u32[]{:S(2)}, u32[]{:S(2)}) collective-permute-start(f32[400,128]{1,0:T(8,128)S(1)} %get-tuple-element.12.sent_even_ref), channel_id=1, source_target_pairs={{0,4},{4,0},{8,12},{12,8},{16,20},{20,16},{24,28},{28,24},{32,36},... | collective-permute-start | bytes 614408 | tf_op jit(solution)/shard_map/ppermute | solution.py:521
  32.5 2.4 %own_steps.1 = (f32[4,8,16,128]{3,2,1,0:T(8,128)S(1)}, f32[288,128]{1,0:T(8,128)S(1)}) custom-call(f32[8,128,128]{2,1,0:T(8,128)S(1)} %get-tuple-element.13.force_ref, f32[128,128]{1,0:T(8,128)S(1)} %get-tuple-element.14.strips_ref, f32[4,128,128]{2,1,0:T(8,128)S(1)} %bitcast.14, f32[2,128,128]{2,1,0:T(8,128)S(1)} %bitcast.17, f32[4,128,128]{2,1,0:T(8,128)S(1)} %bitcast.10), custom_call_target="tpu_custom_call" | custom-call | flops 10000000 | bytes 2000000 | tf_op jit(solution)/shard_map/own_steps/pallas_call | solution.py:523
  34.9 3.7 %collective-permute-done.odd_ref = f32[400,128]{1,0:T(8,128)S(1)} collective-permute-done((f32[400,128]{1,0:T(8,128)S(1)}, f32[400,128]{1,0:T(8,128)S(1)}, u32[]{:S(2)}, u32[]{:S(2)}) %collective-permute-start) | collective-permute-done | bytes 204832 | tf_op jit(solution)/shard_map/ppermute | solution.py:520
  38.6 0.0 collective-permute-done.1.even_ref
  38.6 2.8 %join_bands.1 = f32[4,128,128]{2,1,0:T(8,128)} custom-call(s32[3]{0:T(128)S(1)} %pad_add_fusion.place_ref, f32[400,128]{1,0:T(8,128)S(1)} %collective-permute-done.odd_ref, f32[400,128]{1,0:T(8,128)S(1)} %collective-permute-done.1.even_ref, f32[400,128]{1,0:T(8,128)S(1)} %get-tuple-element.11.sent_odd_ref, f32[400,128]{1,0:T(8,128)S(1)} %get-tuple-element.12.sent_even_ref, ...), custom_call_target="tpu_custom_call" | custom-call | tf_op jit(solution)/shard_map/join_bands/pallas_call | solution.py:533
Async XLA Ops:
  2.3 17.8 %copy-start = (f32[4,16,8,128]{3,2,1,0:T(8,128)S(1)}, f32[4,16,8,128]{3,2,1,0:T(8,128)}, u32[]{:S(2)}) copy-start(f32[4,16,8,128]{3,2,1,0:T(8,128)} %param.8) | copy-start | bytes 786436
  2.3 17.8 %copy-start.1 = (f32[4,16,8,128]{3,2,1,0:T(8,128)S(1)}, f32[4,16,8,128]{3,2,1,0:T(8,128)}, u32[]{:S(2)}) copy-start(f32[4,16,8,128]{3,2,1,0:T(8,128)} %param.6) | copy-start | bytes 786436
  2.3 17.8 %copy-start.2 = (f32[2,16,8,128]{3,2,1,0:T(8,128)S(1)}, f32[2,16,8,128]{3,2,1,0:T(8,128)}, u32[]{:S(2)}) copy-start(f32[2,16,8,128]{3,2,1,0:T(8,128)} %param.7) | copy-start | bytes 393220
  2.3 17.7 %all-to-all-start = ((f32[4,216,128]{2,1,0:T(8,128)}), f32[4,216,128]{2,1,0:T(8,128)S(1)}, u32[]{:S(2)}, u32[]{:S(2)}) async-start(f32[4,216,128]{2,1,0:T(8,128)} %pack_blocks_and_strips.1), calls=%async_computation | async-start | bytes 884736 | tf_op jit(solution)/shard_map/all_to_all | solution.py:503
  21.9 16.7 %collective-permute-start = (f32[400,128]{1,0:T(8,128)S(1)}, f32[400,128]{1,0:T(8,128)S(1)}, u32[]{:S(2)}, u32[]{:S(2)}) collective-permute-start(f32[400,128]{1,0:T(8,128)S(1)} %get-tuple-element.11.sent_odd_ref), channel_id=1, source_target_pairs={{4,8},{8,4},{12,16},{16,12},{20,24},{24,20},{28,32},{32,28},{36,40... | collective-permute-start | bytes 614408 | tf_op jit(solution)/shard_map/ppermute | solution.py:520
  30.6 8.0 %collective-permute-start.1 = (f32[400,128]{1,0:T(8,128)S(1)}, f32[400,128]{1,0:T(8,128)S(1)}, u32[]{:S(2)}, u32[]{:S(2)}) collective-permute-start(f32[400,128]{1,0:T(8,128)S(1)} %get-tuple-element.12.sent_even_ref), channel_id=1, source_target_pairs={{0,4},{4,0},{8,12},{12,8},{16,20},{20,16},{24,28},{28,24},{32,36},... | collective-permute-start | bytes 614408 | tf_op jit(solution)/shard_map/ppermute | solution.py:521

commit v2 on v1

--- a/solution.py
+++ b/solution.py
@@ -13,8 +13,8 @@
 
 TARGET_ROW = 64
 EDGE_ROW = 72
-STRIP_ROW = 136
-LON_ROWS = 216
+STRIP_ROW = 112
+LON_ROWS = 192
 
 A_AT, B_AT, C_AT, STRIP_AT = 16, 18, 19, 23
 LAT_ROWS = 25 * 16
@@ -37,45 +37,69 @@
     return ref[field, pl.ds(first * 8 + row, count, stride=8), :]
 
 
+def pack_blocks(tile, apart, count_ref, column_ref, values_ref, out_ref):
+    slot = lax.broadcasted_iota(jnp.int32, (64, 128), 0)
+    cell = lax.broadcasted_iota(jnp.int32, (64, 128), 0)
+    side = cell >> 3
+    wanted = (cell & 7) * 128 + jnp.where(side < 4, 124 + side, side - 4)
+    lane = lanes_of(8)
+    allowed = (lanes_of(64) < 64) == (side < 4)
+    dest = tile ^ apart
+    left, right = (dest + 3) & 3, (dest + 1) & 3
+    block = lambda t: jnp.where(slot < count_ref[0, t], values_ref[t], 0.0)
+    column = lambda t: column_ref[pl.ds(t, 1), :]
+    out_ref[0:64, :] = block(dest)
+    wide = jnp.concatenate([column(dest), jnp.zeros((1, 64), jnp.int32)], axis=1)
+    out_ref[TARGET_ROW:EDGE_ROW, :] = jnp.broadcast_to(wide.astype(F32), (8, 128))
+    target = jnp.concatenate([column(left), column(right)], axis=1)
+    hit = jnp.where(jnp.logical_and(jnp.broadcast_to(target, (64, 128)) == wanted, allowed), 1.0, 0.0)
+    hit = hit.astype(BF16)
+    both = jnp.concatenate([block(left), block(right)], axis=0)
+    total = jnp.zeros((64, 128), F32)
+    for piece in pieces(both):
+        total = total + jnp.dot(hit, piece, preferred_element_type=F32)
+    at = [total[c * 8 : c * 8 + 8] for c in range(8)]
+    for place, rows in enumerate(
+        (
+            at[3],
+            at[4],
+            jnp.where(lane < 32, pltpu.roll(at[0], 32, 1), at[2]),
+            jnp.where(lane < 32, pltpu.roll(at[7], 32, 1), at[5]),
+            jnp.where(lane < 64, pltpu.roll(at[6], 64, 1), at[1]),
+        )
+    ):
+        out_ref[EDGE_ROW + place * 8 : EDGE_ROW + place * 8 + 8, :] = rows
+
+
+def own_blocks_kernel(count_ref, column_ref, values_ref, out_ref):
+    pack_blocks(lax.axis_index("lon"), 0, count_ref, column_ref, values_ref, out_ref)
+
+
 def pack_kernel(*refs):
-    sources, out_ref, copies_of, sems = refs[:6], refs[6], refs[7:13], refs[13]
+    sources, outs, copies_of, packed, strips_ref, sems = (
+        refs[:6], refs[6:9], refs[9:15], refs[15:18], refs[18], refs[19]
+    )
     copies = [pltpu.make_async_copy(sources[i], copies_of[i], sems.at[i]) for i in range(6)]
-    for copy in copies:
-        copy.start()
+    for i in (2, 1, 0, 3, 5, 4):
+        copies[i].start()
     for copy in copies[:3]:
         copy.wait()
     count_ref, column_ref, values_ref, lam_ref, winds_ref, coupling_ref = copies_of
-    slot = lax.broadcasted_iota(jnp.int32, (64, 128), 0)
-    blocks = []
-    columns = []
-    for tile in range(4):
-        block = jnp.where(slot < count_ref[0, tile], values_ref[tile], 0.0)
-        blocks.append(block)
-        column = column_ref[tile : tile + 1, :]
-        columns.append(column)
-        out_ref[tile, 0:64, :] = block
-        wide = jnp.concatenate([column, jnp.zeros((1, 64), jnp.int32)], axis=1)
-        out_ref[tile, TARGET_ROW:EDGE_ROW, :] = jnp.broadcast_to(wide.astype(F32), (8, 128))
-
-    cell = lax.broadcasted_iota(jnp.int32, (64, 128), 0)
-    side = cell & 7
-    wanted = (cell >> 3) * 128 + jnp.where(side < 4, 124 + side, side - 4)
-    allowed = (lanes_of(64) < 64) == (side < 4)
-    for tile in range(4):
-        left, right = (tile + 3) % 4, (tile + 1) % 4
-        target = jnp.concatenate([columns[left], columns[right]], axis=1)
-        hit = jnp.where(jnp.logical_and(jnp.broadcast_to(target, (64, 128)) == wanted, allowed), 1.0, 0.0)
-        hit = hit.astype(BF16)
-        both = jnp.concatenate([blocks[left], blocks[right]], axis=0)
-        total = jnp.zeros((64, 128), F32)
-        for piece in pieces(both):
-            total = total + jnp.dot(hit, piece, preferred_element_type=F32)
-        out_ref[tile, EDGE_ROW:STRIP_ROW, :] = total
+    tile = lax.axis_index("lon")
+    lane = lanes_of(8)
+    sent = []
+    for apart in (3, 2, 1):
+        pack_blocks(tile, apart, count_ref, column_ref, values_ref, packed[apart - 1])
+        sent.append(
+            pltpu.make_async_copy(
+                packed[apart - 1], outs[apart - 1].at[pl.ds(0, STRIP_ROW), :], sems.at[5 + apart]
+            )
+        )
+        sent[-1].start()
 
     for copy in copies[3:]:
         copy.wait()
-    lane = lanes_of(8)
-    row = STRIP_ROW
+    row = 0
     for ref, fields in ((lam_ref, 4), (winds_ref, 2), (coupling_ref, 4)):
         for field in range(fields):
             strip = jnp.zeros((8, 128), F32)
@@ -84,9 +108,17 @@
                     at = half * 64 + r * 8
                     moved = pltpu.roll(levels(ref, field, r, half * 8, 8), (at + 4) % 128, 1)
                     strip = jnp.where(jnp.logical_and(lane >= at, lane < at + 8), moved, strip)
-            for tile in range(4):
-                out_ref[tile, row : row + 8, :] = strip
+            strips_ref[row : row + 8, :] = strip
             row += 8
+    for apart in (3, 1):
+        sent.append(
+            pltpu.make_async_copy(
+                strips_ref, outs[apart - 1].at[pl.ds(STRIP_ROW, LON_ROWS - STRIP_ROW), :], sems.at[8 + apart]
+            )
+        )
+        sent[-1].start()
+    for copy in sent:
+        copy.wait()
 
 
 def strip_lane(plane, way):
@@ -198,16 +230,19 @@
         keep(step, u, strips)
 
 
-def halo_kernel(place_ref, got_ref, lam_ref, winds_ref, coupling_ref, even_ref, odd_ref, force_ref, strips_ref):
-    is_even = lax.rem(place_ref[0], 2) == 0
-    tile = place_ref[1]
+def halo_kernel(
+    got3_ref, got2_ref, got1_ref, own_ref, lam_ref, winds_ref, coupling_ref, even_ref, odd_ref, force_ref, strips_ref, edge_ref
+):
+    is_even = lax.rem(lax.axis_index("lat"), 2) == 0
+    right_is_1 = lax.rem(lax.axis_index("lon"), 2) == 0
     lane = lanes_of(8)
     lane1 = lanes_of(1)
-
-    rows = [got_ref[s, TARGET_ROW : TARGET_ROW + 1, :] for s in range(4)]
+    messages = (own_ref, got1_ref, got2_ref, got3_ref)
+
+    rows = [message[TARGET_ROW : TARGET_ROW + 1, :] for message in messages]
     halves = [jnp.where(lane1 < 64, rows[s], pltpu.roll(rows[s + 1], 64, 1)) for s in (0, 2)]
     target = jnp.concatenate(halves, axis=1).astype(jnp.int32)
-    blocks = jnp.concatenate([got_ref[s, 0:64, :] for s in range(4)], axis=0)
+    blocks = jnp.concatenate([message[0:64, :] for message in messages], axis=0)
     stacked = jnp.concatenate(pieces(blocks.T), axis=0)
     cell = lax.broadcasted_iota(jnp.int32, (256, 256), 0)
     for pair in range(4):
@@ -217,20 +252,34 @@
         force_ref[2 * pair] = both[:, 0:128]
         force_ref[2 * pair + 1] = both[:, 128:256]
 
-    edge = got_ref[0, EDGE_ROW:STRIP_ROW, :]
-    for s in range(1, 4):
-        edge = edge + got_ref[s, EDGE_ROW:STRIP_ROW, :]
-    edge = jnp.concatenate([edge, edge], axis=0).T
+    near2, near1, far24, far42, thirds = [
+        sum(message[EDGE_ROW + place * 8 : EDGE_ROW + place * 8 + 8, :] for message in messages)
+        for place in (0, 1, 2, 3, 4)
+    ]
+    for c, rows in enumerate(
+        (
+            jnp.where(lane >= 96, pltpu.roll(far24, 96, 1), 0.0),
+            jnp.where(lane >= 64, thirds, 0.0),
+            jnp.where(lane >= 32, far24, 0.0),
+            near2,
+            near1,
+            jnp.where(lane >= 32, far42, 0.0),
+            jnp.where(lane >= 64, pltpu.roll(thirds, 64, 1), 0.0),
+            jnp.where(lane >= 96, pltpu.roll(far42, 96, 1), 0.0),
+        )
+    ):
+        edge_ref[pl.ds(c, 8, stride=8), :] = rows
+        edge_ref[pl.ds(64 + c, 8, stride=8), :] = rows
+    edge = edge_ref[...].T
 
     def edge_strip(instant, field):
         at = instant * 32 + field * 16
         return jnp.where(lane < 64, edge[at : at + 8], edge[at + 8 : at + 16])
 
-    left = lax.rem(tile + 3, 4)
-    right = lax.rem(tile + 1, 4)
+    from_1 = ((lane & 7) < 4) != right_is_1
     for field in range(10):
         at = STRIP_ROW + field * 8
-        strip = jnp.where((lane & 7) < 4, got_ref[left, at : at + 8, :], got_ref[right, at : at + 8, :])
+        strip = jnp.where(from_1, got1_ref[at : at + 8, :], got3_ref[at : at + 8, :])
         if field in (2, 3):
             strip = strip + edge_strip(3, field - 2)
         strips_ref[field * 8 : field * 8 + 8, :] = strip
@@ -311,7 +360,7 @@
 
 
 def join_kernel(
-    place_ref,
+    bands,
     odd_ref,
     even_ref,
     sent_odd_ref,
@@ -323,10 +372,10 @@
     out_ref,
     border_ref,
 ):
-    band = place_ref[0]
+    band = lax.axis_index("lat")
     is_even = lax.rem(band, 2) == 0
     low_mask = jnp.where(band > 0, 1.0, 0.0).astype(F32)
-    high_mask = jnp.where(band < place_ref[2] - 1, 1.0, 0.0).astype(F32)
+    high_mask = jnp.where(band < bands - 1, 1.0, 0.0).astype(F32)
     lane = lanes_of(8)
     side = lane & 7
     strip_row = (lane >> 3) - 2
@@ -468,9 +517,6 @@
     return [pl.BlockSpec(memory_space=pltpu.VMEM)] * count
 
 
-SMEM = pl.BlockSpec(memory_space=pltpu.SMEM)
-
-
 def params(mebibytes=24):
     return pltpu.CompilerParams(vmem_limit_bytes=mebibytes * 1024 * 1024)
 
@@ -481,13 +527,13 @@
     lam = lam_end.reshape(4, 128, 128)
     wind = winds.reshape(2, 128, 128)
     couple = coupling.reshape(4, 128, 128)
-    place = jnp.stack([lax.axis_index("lat"), lax.axis_index("lon"), jnp.int32(bands)]).astype(jnp.int32)
-
-    message = pl.pallas_call(
+
+    lon_rows = (LON_ROWS, STRIP_ROW, LON_ROWS)
+    parts = pl.pallas_call(
         pack_kernel,
-        out_shape=jax.ShapeDtypeStruct((tiles, LON_ROWS, 128), F32),
+        out_shape=tuple(jax.ShapeDtypeStruct((rows, 128), F32) for rows in lon_rows),
         in_specs=[pl.BlockSpec(memory_space=pltpu.HBM)] * 6,
-        out_specs=vmem(1)[0],
+        out_specs=tuple([pl.BlockSpec(memory_space=pltpu.HBM)] * 3),
         scratch_shapes=[
             pltpu.SMEM((1, 4), jnp.int32),
             pltpu.VMEM((4, 64), jnp.int32),
@@ -495,12 +541,28 @@
             pltpu.VMEM((4, 128, 128), F32),
             pltpu.VMEM((2, 128, 128), F32),
             pltpu.VMEM((4, 128, 128), F32),
-            pltpu.SemaphoreType.DMA((6,)),
+            pltpu.VMEM((STRIP_ROW, 128), F32),
+            pltpu.VMEM((STRIP_ROW, 128), F32),
+            pltpu.VMEM((STRIP_ROW, 128), F32),
+            pltpu.VMEM((LON_ROWS - STRIP_ROW, 128), F32),
+            pltpu.SemaphoreType.DMA((12,)),
         ],
         compiler_params=params(60),
         name="pack_blocks_and_strips",
     )(obs_count, obs_column[0], obs_values[0], lam, wind, couple)
-    got = lax.all_to_all(message, "lon", split_axis=0, concat_axis=0, tiled=True)
+    got3, got2, got1 = [
+        lax.ppermute(parts[apart - 1], "lon", [(i, i ^ apart) for i in range(tiles)]) for apart in (3, 2, 1)
+    ]
+
+    own_part = pl.pallas_call(
+        own_blocks_kernel,
+        out_shape=jax.ShapeDtypeStruct((STRIP_ROW, 128), F32),
+        in_specs=[pl.BlockSpec(memory_space=pltpu.SMEM)] + vmem(2),
+        out_specs=vmem(1)[0],
+        compiler_params=params(),
+        cost_estimate=pl.CostEstimate(flops=5_000_000, bytes_accessed=1_000_000, transcendentals=0),
+        name="own_blocks",
+    )(obs_count, obs_column[0], obs_values[0])
 
     halo = jax.ShapeDtypeStruct((LAT_ROWS, 128), F32)
     even, odd, force, strips = pl.pallas_call(
@@ -511,11 +573,12 @@
             jax.ShapeDtypeStruct((8, 128, 128), F32),
             jax.ShapeDtypeStruct((128, 128), F32),
         ),
-        in_specs=[SMEM] + vmem(4),
+        in_specs=vmem(7),
         out_specs=tuple(vmem(4)),
+        scratch_shapes=[pltpu.VMEM((128, 128), F32)],
         compiler_params=params(),
         name="scatter_and_halo",
-    )(place, got, lam, wind, couple)
+    )(got3, got2, got1, own_part, lam, wind, couple)
     swap = lambda first: [p for i in range(first, bands - 1, 2) for p in ((i, i + 1), (i + 1, i))]
     got_odd = lax.ppermute(odd, "lat", swap(1))
     got_even = lax.ppermute(even, "lat", swap(0))
@@ -531,14 +594,14 @@
     )(force, strips, lam, wind, couple)
 
     out = pl.pallas_call(
-        join_kernel,
+        functools.partial(join_kernel, bands),
         out_shape=jax.ShapeDtypeStruct((4, 128, 128), F32),
-        in_specs=[SMEM] + vmem(8),
+        in_specs=vmem(8),
         out_specs=vmem(1)[0],
         scratch_shapes=[pltpu.VMEM((192, 128), F32)],
         compiler_params=params(),
         name="join_bands",
-    )(place, got_odd, got_even, odd, even, own, wide, wind, couple)
+    )(got_odd, got_even, odd, even, own, wide, wind, couple)
     return out.reshape(lam_end.shape)
 
 

time: 41.6 us -> 38.1 us (0.916)
  the two profiles are of different devices: /device:TPU:512 before, /device:TPU:520 now
where the time goes in v2:
time: 38.1 us; the launch traced here: 37.9 us
  starting transfers between devices  18 us (47%)
  waiting for transfers between devices  10.7 us (28%)
  Pallas kernels  9.01 us (24%)
    ppermute x3, starting transfers between devices, body(): lax.ppermute(parts[apart - 1], 'lon', [(i, i ^ apart) for i in range(tile...  9.92 us
    ppermute x1, waiting for transfers between devices, body(): got_odd = lax.ppermute(odd, 'lat', swap(1))  6.25 us
    ppermute x1, starting transfers between devices, body(): got_odd = lax.ppermute(odd, 'lat', swap(1))  6.16 us
    ppermute x3, waiting for transfers between devices, body(): lax.ppermute(parts[apart - 1], 'lon', [(i, i ^ apart) for i in range(tile...  4.44 us
    pallas_call x1, Pallas kernels, body(): pl.pallas_call(own_kernel, out_shape=(jax.ShapeDtypeStruct((4, 8, 16, 128...  2.41 us
    pallas_call x1, Pallas kernels, body(): pl.pallas_call(pack_kernel, out_shape=tuple((jax.ShapeDtypeStruct((rows,...  2.31 us
    pallas_call x1, Pallas kernels, body(): pl.pallas_call(functools.partial(join_kernel, bands), out_shape=jax.Shape...  2.17 us
    ppermute x1, starting transfers between devices, body(): got_even = lax.ppermute(even, 'lat', swap(0))  1.92 us
  transfers between devices with their start and end apart: 5, of which 2 were waited for; matrix products, arithmetic and copies ran while one was open for 0% of the time, Pallas kernels for 8%

profile of v2, /device:TPU:520, one launch (start us, length us, event | category | flops | bytes accessed | tf_op | source)
XLA Modules:
  0.0 37.9 jit_solution(10920277548091868943)
XLA Ops:
  0.0 0.0 copy-start.3
  0.0 0.0 copy-start.4
  0.0 0.0 copy-start.5
  0.0 0.0 copy-start
  0.0 0.0 copy-start.1
  0.0 2.3 %pack_blocks_and_strips.1 = (f32[192,128]{1,0:T(8,128)}, f32[112,128]{1,0:T(8,128)}, f32[192,128]{1,0:T(8,128)}) custom-call(s32[1,4]{1,0:T(1,128)} %count_ref.1, s32[4,64]{1,0:T(4,128)} %bitcast.19, f32[4,64,128]{2,1,0:T(8,128)} %bitcast.17, f32[4,128,128]{2,1,0:T(8,128)} %bitcast.10, f32[2,128,128]{2,1,0:T(8,128)} %bitcast.13, f32[4,128,128]{2,1,0:T(8,128)} %bitcast.6), custom_call_target="tpu_custom_call" | custom-call | tf_op jit(solution)/shard_map/pack_blocks_and_strips/pallas_call | solution.py:532
  2.3 0.0 copy-start.2
  2.4 3.6 %collective-permute-start = (f32[192,128]{1,0:T(8,128)}, f32[192,128]{1,0:T(8,128)S(1)}, u32[]{:S(2)}, u32[]{:S(2)}) collective-permute-start(f32[192,128]{1,0:T(8,128)} %get-tuple-element.14), channel_id=1, source_target_pairs={{0,3},{1,2},{2,1},{3,0},{4,7},{5,6},{6,5},{7,4},{8,11},{9,10},{10,... | collective-permute-start | bytes 294920 | tf_op jit(solution)/shard_map/ppermute | solution.py:554
  6.0 4.4 %collective-permute-start.2 = (f32[192,128]{1,0:T(8,128)}, f32[192,128]{1,0:T(8,128)S(1)}, u32[]{:S(2)}, u32[]{:S(2)}) collective-permute-start(f32[192,128]{1,0:T(8,128)} %get-tuple-element.16), channel_id=1, source_target_pairs={{0,1},{1,0},{2,3},{3,2},{4,5},{5,4},{6,7},{7,6},{8,9},{9,8},{10,11... | collective-permute-start | bytes 294920 | tf_op jit(solution)/shard_map/ppermute | solution.py:554
  10.4 1.9 %collective-permute-start.1 = (f32[112,128]{1,0:T(8,128)}, f32[112,128]{1,0:T(8,128)S(1)}, u32[]{:S(2)}, u32[]{:S(2)}) collective-permute-start(f32[112,128]{1,0:T(8,128)} %get-tuple-element.15), channel_id=1, source_target_pairs={{0,2},{1,3},{2,0},{3,1},{4,6},{5,7},{6,4},{7,5},{8,10},{9,11},{10,... | collective-permute-start | bytes 172040 | tf_op jit(solution)/shard_map/ppermute | solution.py:554
  12.3 0.0 copy-done.3
  12.3 0.0 copy-done.4
  12.3 0.0 copy-done.5
  12.3 0.8 %own_blocks.1.own_ref = f32[112,128]{1,0:T(8,128)S(1)} custom-call(s32[1,4]{1,0:T(1,128)S(1)} %copy-done.5, s32[4,64]{1,0:T(4,128)S(1)} %bitcast.20, f32[4,64,128]{2,1,0:T(8,128)S(1)} %bitcast.18), custom_call_target="tpu_custom_call" | custom-call | flops 5000000 | bytes 1000000 | tf_op jit(solution)/shard_map/own_blocks/pallas_call | solution.py:557
  13.1 4.4 %collective-permute-done.1.got2_ref = f32[112,128]{1,0:T(8,128)S(1)} collective-permute-done((f32[112,128]{1,0:T(8,128)}, f32[112,128]{1,0:T(8,128)S(1)}, u32[]{:S(2)}, u32[]{:S(2)}) %collective-permute-start.1) | collective-permute-done | bytes 57376 | tf_op jit(solution)/shard_map/ppermute | solution.py:554
  17.6 0.0 collective-permute-done.got3_ref
  17.6 0.0 collective-permute-done.2.got1_ref
  17.6 0.0 copy-done
  17.6 0.0 copy-done.1
  17.6 0.0 copy-done.2
  17.6 1.3 %scatter_and_halo.1 = (f32[400,128]{1,0:T(8,128)S(1)}, f32[400,128]{1,0:T(8,128)S(1)}, f32[8,128,128]{2,1,0:T(8,128)S(1)}, f32[128,128]{1,0:T(8,128)S(1)}) custom-call(f32[192,128]{1,0:T(8,128)S(1)} %collective-permute-done.got3_ref, f32[112,128]{1,0:T(8,128)S(1)} %collective-permute-done.1.got2_ref, f32[192,128]{1,0:T(8,128)S(1)} %collective-permute-done.2.got1_ref, ...), custom_call_target="tpu_custom_call" | custom-call | tf_op jit(solution)/shard_map/scatter_and_halo/pallas_call | solution.py:568
  18.9 6.2 %collective-permute-start.3 = (f32[400,128]{1,0:T(8,128)S(1)}, f32[400,128]{1,0:T(8,128)S(1)}, u32[]{:S(2)}, u32[]{:S(2)}) collective-permute-start(f32[400,128]{1,0:T(8,128)S(1)} %get-tuple-element.17.sent_odd_ref), channel_id=1, source_target_pairs={{4,8},{8,4},{12,16},{16,12},{20,24},{24,20},{28,32},{32,28},{36,40... | collective-permute-start | bytes 614408 | tf_op jit(solution)/shard_map/ppermute | solution.py:583
  25.1 1.9 %collective-permute-start.4 = (f32[400,128]{1,0:T(8,128)S(1)}, f32[400,128]{1,0:T(8,128)S(1)}, u32[]{:S(2)}, u32[]{:S(2)}) collective-permute-start(f32[400,128]{1,0:T(8,128)S(1)} %get-tuple-element.18.sent_even_ref), channel_id=1, source_target_pairs={{0,4},{4,0},{8,12},{12,8},{16,20},{20,16},{24,28},{28,24},{32,36},... | collective-permute-start | bytes 614408 | tf_op jit(solution)/shard_map/ppermute | solution.py:584
  27.0 2.4 %own_steps.1 = (f32[4,8,16,128]{3,2,1,0:T(8,128)S(1)}, f32[288,128]{1,0:T(8,128)S(1)}) custom-call(f32[8,128,128]{2,1,0:T(8,128)S(1)} %get-tuple-element.19.force_ref, f32[128,128]{1,0:T(8,128)S(1)} %get-tuple-element.20.strips_ref, f32[4,128,128]{2,1,0:T(8,128)S(1)} %bitcast.12, f32[2,128,128]{2,1,0:T(8,128)S(1)} %bitcast.15, f32[4,128,128]{2,1,0:T(8,128)S(1)} %bitcast.8), custom_call_target="tpu_custom_call" | custom-call | flops 10000000 | bytes 2000000 | tf_op jit(solution)/shard_map/own_steps/pallas_call | solution.py:586
  29.4 6.2 %collective-permute-done.3.odd_ref = f32[400,128]{1,0:T(8,128)S(1)} collective-permute-done((f32[400,128]{1,0:T(8,128)S(1)}, f32[400,128]{1,0:T(8,128)S(1)}, u32[]{:S(2)}, u32[]{:S(2)}) %collective-permute-start.3) | collective-permute-done | bytes 204832 | tf_op jit(solution)/shard_map/ppermute | solution.py:583
  35.7 0.0 collective-permute-done.4.even_ref
  35.7 2.2 %join_bands.1 = f32[4,128,128]{2,1,0:T(8,128)} custom-call(f32[400,128]{1,0:T(8,128)S(1)} %collective-permute-done.3.odd_ref, f32[400,128]{1,0:T(8,128)S(1)} %collective-permute-done.4.even_ref, f32[400,128]{1,0:T(8,128)S(1)} %get-tuple-element.17.sent_odd_ref, f32[400,128]{1,0:T(8,128)S(1)} %get-tuple-element.18.sent_even_ref, ...), custom_call_target="tpu_custom_call" | custom-call | tf_op jit(solution)/shard_map/join_bands/pallas_call | solution.py:596
Async XLA Ops:
  0.0 12.3 %copy-start.3 = (f32[1,4,64,128]{3,2,1,0:T(8,128)S(1)}, f32[1,4,64,128]{3,2,1,0:T(8,128)}, u32[]{:S(2)}) copy-start(f32[1,4,64,128]{3,2,1,0:T(8,128)} %param.9) | copy-start | bytes 393220
  0.0 12.3 %copy-start.4 = (s32[1,4,64]{2,1,0:T(4,128)S(1)}, s32[1,4,64]{2,1,0:T(4,128)}, u32[]{:S(2)}) copy-start(s32[1,4,64]{2,1,0:T(4,128)} %param.10) | copy-start | bytes 3076
  0.0 12.3 %copy-start.5 = (s32[1,4]{1,0:T(1,128)S(1)}, s32[1,4]{1,0:T(1,128)}, u32[]{:S(2)}) copy-start(s32[1,4]{1,0:T(1,128)} %count_ref.1) | copy-start | bytes 52
  0.0 17.5 %copy-start = (f32[4,16,8,128]{3,2,1,0:T(8,128)S(1)}, f32[4,16,8,128]{3,2,1,0:T(8,128)}, u32[]{:S(2)}) copy-start(f32[4,16,8,128]{3,2,1,0:T(8,128)} %param.8) | copy-start | bytes 786436
  0.0 17.5 %copy-start.1 = (f32[4,16,8,128]{3,2,1,0:T(8,128)S(1)}, f32[4,16,8,128]{3,2,1,0:T(8,128)}, u32[]{:S(2)}) copy-start(f32[4,16,8,128]{3,2,1,0:T(8,128)} %param.6) | copy-start | bytes 786436
  2.3 15.2 %copy-start.2 = (f32[2,16,8,128]{3,2,1,0:T(8,128)S(1)}, f32[2,16,8,128]{3,2,1,0:T(8,128)}, u32[]{:S(2)}) copy-start(f32[2,16,8,128]{3,2,1,0:T(8,128)} %param.7) | copy-start | bytes 393220
  2.4 15.2 %collective-permute-start = (f32[192,128]{1,0:T(8,128)}, f32[192,128]{1,0:T(8,128)S(1)}, u32[]{:S(2)}, u32[]{:S(2)}) collective-permute-start(f32[192,128]{1,0:T(8,128)} %get-tuple-element.14), channel_id=1, source_target_pairs={{0,3},{1,2},{2,1},{3,0},{4,7},{5,6},{6,5},{7,4},{8,11},{9,10},{10,... | collective-permute-start | bytes 294920 | tf_op jit(solution)/shard_map/ppermute | solution.py:554
  6.0 11.6 %collective-permute-start.2 = (f32[192,128]{1,0:T(8,128)}, f32[192,128]{1,0:T(8,128)S(1)}, u32[]{:S(2)}, u32[]{:S(2)}) collective-permute-start(f32[192,128]{1,0:T(8,128)} %get-tuple-element.16), channel_id=1, source_target_pairs={{0,1},{1,0},{2,3},{3,2},{4,5},{5,4},{6,7},{7,6},{8,9},{9,8},{10,11... | collective-permute-start | bytes 294920 | tf_op jit(solution)/shard_map/ppermute | solution.py:554
  10.4 7.2 %collective-permute-start.1 = (f32[112,128]{1,0:T(8,128)}, f32[112,128]{1,0:T(8,128)S(1)}, u32[]{:S(2)}, u32[]{:S(2)}) collective-permute-start(f32[112,128]{1,0:T(8,128)} %get-tuple-element.15), channel_id=1, source_target_pairs={{0,2},{1,3},{2,0},{3,1},{4,6},{5,7},{6,4},{7,5},{8,10},{9,11},{10,... | collective-permute-start | bytes 172040 | tf_op jit(solution)/shard_map/ppermute | solution.py:554
  18.9 16.8 %collective-permute-start.3 = (f32[400,128]{1,0:T(8,128)S(1)}, f32[400,128]{1,0:T(8,128)S(1)}, u32[]{:S(2)}, u32[]{:S(2)}) collective-permute-start(f32[400,128]{1,0:T(8,128)S(1)} %get-tuple-element.17.sent_odd_ref), channel_id=1, source_target_pairs={{4,8},{8,4},{12,16},{16,12},{20,24},{24,20},{28,32},{32,28},{36,40... | collective-permute-start | bytes 614408 | tf_op jit(solution)/shard_map/ppermute | solution.py:583
  25.1 10.6 %collective-permute-start.4 = (f32[400,128]{1,0:T(8,128)S(1)}, f32[400,128]{1,0:T(8,128)S(1)}, u32[]{:S(2)}, u32[]{:S(2)}) collective-permute-start(f32[400,128]{1,0:T(8,128)S(1)} %get-tuple-element.18.sent_even_ref), channel_id=1, source_target_pairs={{0,4},{4,0},{8,12},{12,8},{16,20},{20,16},{24,28},{28,24},{32,36},... | collective-permute-start | bytes 614408 | tf_op jit(solution)/shard_map/ppermute | solution.py:584

commit v3 on v2

--- a/solution.py
+++ b/solution.py
@@ -76,9 +76,7 @@
 
 
 def pack_kernel(*refs):
-    sources, outs, copies_of, packed, strips_ref, sems = (
-        refs[:6], refs[6:9], refs[9:15], refs[15:18], refs[18], refs[19]
-    )
+    sources, outs, copies_of, sems = refs[:6], refs[6:9], refs[9:15], refs[15]
     copies = [pltpu.make_async_copy(sources[i], copies_of[i], sems.at[i]) for i in range(6)]
     for i in (2, 1, 0, 3, 5, 4):
         copies[i].start()
@@ -87,19 +85,12 @@
     count_ref, column_ref, values_ref, lam_ref, winds_ref, coupling_ref = copies_of
     tile = lax.axis_index("lon")
     lane = lanes_of(8)
-    sent = []
     for apart in (3, 2, 1):
-        pack_blocks(tile, apart, count_ref, column_ref, values_ref, packed[apart - 1])
-        sent.append(
-            pltpu.make_async_copy(
-                packed[apart - 1], outs[apart - 1].at[pl.ds(0, STRIP_ROW), :], sems.at[5 + apart]
-            )
-        )
-        sent[-1].start()
+        pack_blocks(tile, apart, count_ref, column_ref, values_ref, outs[apart - 1])
 
     for copy in copies[3:]:
         copy.wait()
-    row = 0
+    row = STRIP_ROW
     for ref, fields in ((lam_ref, 4), (winds_ref, 2), (coupling_ref, 4)):
         for field in range(fields):
             strip = jnp.zeros((8, 128), F32)
@@ -108,17 +99,9 @@
                     at = half * 64 + r * 8
                     moved = pltpu.roll(levels(ref, field, r, half * 8, 8), (at + 4) % 128, 1)
                     strip = jnp.where(jnp.logical_and(lane >= at, lane < at + 8), moved, strip)
-            strips_ref[row : row + 8, :] = strip
+            for apart in (1, 3):
+                outs[apart - 1][row : row + 8, :] = strip
             row += 8
-    for apart in (3, 1):
-        sent.append(
-            pltpu.make_async_copy(
-                strips_ref, outs[apart - 1].at[pl.ds(STRIP_ROW, LON_ROWS - STRIP_ROW), :], sems.at[8 + apart]
-            )
-        )
-        sent[-1].start()
-    for copy in sent:
-        copy.wait()
 
 
 def strip_lane(plane, way):
@@ -138,20 +121,21 @@
 
 def along(x, to_left, to_right, beside, at, lane):
     p_right, p_left = to_left * x, to_right * x
-    edge = pltpu.roll(beside, (128 - (at + 4)) % 128, 1)
-    right = jnp.where(lane == 127, edge, pltpu.roll(p_right, 127, 1))
-    left = jnp.where(lane == 0, edge, pltpu.roll(p_left, 1, 1))
-    return right + left, jnp.where(lane == 0, p_right, p_left)
+    strip_right, strip_left = beside
+    right = jnp.where(lane == 127, pltpu.roll(strip_right, (123 - at) % 128, 1), pltpu.roll(p_right, 127, 1))
+    left = jnp.where(lane == 0, pltpu.roll(strip_left, (125 - at) % 128, 1), pltpu.roll(p_left, 1, 1))
+    return right + left, (p_right, p_left)
 
 
 def insert(inner, pair, at, lane):
-    moved = pltpu.roll(pair, (at + 4) % 128, 1)
-    return jnp.where(jnp.logical_or(lane == at + 4, lane == at + 3), moved, inner)
+    p_right, p_left = pair
+    inner = jnp.where(lane == at + 3, pltpu.roll(p_right, (at + 3) % 128, 1), inner)
+    return jnp.where(lane == at + 4, pltpu.roll(p_left, (at + 5) % 128, 1), inner)
 
 
 def strip_along(rolled_right, rolled_left, inner, side):
-    right = jnp.where(side == 3, pltpu.roll(inner, 127, 1), rolled_right)
-    left = jnp.where(side == 4, pltpu.roll(inner, 1, 1), rolled_left)
+    right = jnp.where(side == 3, inner, rolled_right)
+    left = jnp.where(side == 4, inner, rolled_left)
     return right + left
 
 
@@ -193,10 +177,10 @@
         later_strips = []
         for field in range(4):
             x = u[field]
-            rolled_right = pltpu.roll(strip_right * strips[field], 127, 1)
-            rolled_left = pltpu.roll(strip_left * strips[field], 1, 1)
-            beside = jnp.where(side == 3, rolled_right, rolled_left)
-            inner = beside
+            beside = (strip_right * strips[field], strip_left * strips[field])
+            rolled_right = pltpu.roll(beside[0], 127, 1)
+            rolled_left = pltpu.roll(beside[1], 1, 1)
+            inner = beside[0]
             for half in range(2):
                 for row in rows:
                     at = half * 64 + row * 8
@@ -452,10 +436,10 @@
             for half in range(2):
                 xs = strips[field][half]
                 if step > 0:
-                    rolled_right = pltpu.roll((DIFFUSION + strip_b[half]) * xs, 127, 1)
-                    rolled_left = pltpu.roll((DIFFUSION - strip_b[half]) * xs, 1, 1)
-                    beside = jnp.where(side == 3, rolled_right, rolled_left)
-                    inner = beside
+                    beside = ((DIFFUSION + strip_b[half]) * xs, (DIFFUSION - strip_b[half]) * xs)
+                    rolled_right = pltpu.roll(beside[0], 127, 1)
+                    rolled_left = pltpu.roll(beside[1], 1, 1)
+                    inner = beside[0]
                 for row in rows:
                     terms = []
                     if (row, half) in x:
@@ -533,7 +517,7 @@
         pack_kernel,
         out_shape=tuple(jax.ShapeDtypeStruct((rows, 128), F32) for rows in lon_rows),
         in_specs=[pl.BlockSpec(memory_space=pltpu.HBM)] * 6,
-        out_specs=tuple([pl.BlockSpec(memory_space=pltpu.HBM)] * 3),
+        out_specs=tuple(vmem(3)),
         scratch_shapes=[
             pltpu.SMEM((1, 4), jnp.int32),
             pltpu.VMEM((4, 64), jnp.int32),
@@ -541,13 +525,9 @@
             pltpu.VMEM((4, 128, 128), F32),
             pltpu.VMEM((2, 128, 128), F32),
             pltpu.VMEM((4, 128, 128), F32),
-            pltpu.VMEM((STRIP_ROW, 128), F32),
-            pltpu.VMEM((STRIP_ROW, 128), F32),
-            pltpu.VMEM((STRIP_ROW, 128), F32),
-            pltpu.VMEM((LON_ROWS - STRIP_ROW, 128), F32),
-            pltpu.SemaphoreType.DMA((12,)),
+            pltpu.SemaphoreType.DMA((6,)),
         ],
-        compiler_params=params(60),
+        compiler_params=pltpu.CompilerParams(vmem_limit_bytes=54950 * 1024),
         name="pack_blocks_and_strips",
     )(obs_count, obs_column[0], obs_values[0], lam, wind, couple)
     got3, got2, got1 = [

time: 38.1 us -> 37.2 us (0.976)
  Pallas kernels: 9.01 us -> 7.02 us
  local copies, waits for them, and re-layouts: 0.03 us -> 0.7 us
  waiting for transfers between devices: 10.7 us -> 11.1 us
    pallas_call x1, Pallas kernels: 2.31 us -> 1.62 us  [body(): pl.pallas_call(pack_kernel, out_shape=tuple((jax.ShapeDtypeStruct((rows,...]
    unnamed x12, local copies, waits for them, and re-layouts: 0.03 us -> 0.7 us
    ppermute x1, waiting for transfers between devices: 6.25 us -> 6.86 us  [body(): got_odd = lax.ppermute(odd, 'lat', swap(1))]
    pallas_call x1, Pallas kernels: 2.41 us -> 1.8 us  [body(): pl.pallas_call(own_kernel, out_shape=(jax.ShapeDtypeStruct((4, 8, 16, 128...]
    pallas_call x1, Pallas kernels: 2.17 us -> 1.73 us  [body(): pl.pallas_call(functools.partial(join_kernel, bands), out_shape=jax.Shape...]
  transfers between devices with their start and end apart: 5 -> 5, of which waited for: 2 -> 2; matrix products, arithmetic and copies ran while one was open for 0% -> 0% of each run, Pallas kernels for 8% -> 7%
where the time goes in v3:
time: 37.2 us; the launch traced here: 36.9 us
  starting transfers between devices  18 us (48%)
  waiting for transfers between devices  11.1 us (30%)
  Pallas kernels  7.02 us (19%)
  local copies, waits for them, and re-layouts  0.7 us (2%)
    ppermute x3, starting transfers between devices, body(): lax.ppermute(parts[apart - 1], 'lon', [(i, i ^ apart) for i in range(tile...  9.92 us
    ppermute x1, waiting for transfers between devices, body(): got_odd = lax.ppermute(odd, 'lat', swap(1))  6.86 us
    ppermute x1, starting transfers between devices, body(): got_odd = lax.ppermute(odd, 'lat', swap(1))  6.16 us
    ppermute x3, waiting for transfers between devices, body(): lax.ppermute(parts[apart - 1], 'lon', [(i, i ^ apart) for i in range(tile...  4.25 us
    ppermute x1, starting transfers between devices, body(): got_even = lax.ppermute(even, 'lat', swap(0))  1.92 us
    pallas_call x1, Pallas kernels, body(): pl.pallas_call(own_kernel, out_shape=(jax.ShapeDtypeStruct((4, 8, 16, 128...  1.8 us
    pallas_call x1, Pallas kernels, body(): pl.pallas_call(functools.partial(join_kernel, bands), out_shape=jax.Shape...  1.73 us
    pallas_call x1, Pallas kernels, body(): pl.pallas_call(pack_kernel, out_shape=tuple((jax.ShapeDtypeStruct((rows,...  1.62 us
  transfers between devices with their start and end apart: 5, of which 2 were waited for; matrix products, arithmetic and copies ran while one was open for 0% of the time, Pallas kernels for 7%

profile of v3, /device:TPU:520, one launch (start us, length us, event | category | flops | bytes accessed | tf_op | source)
XLA Modules:
  0.0 36.9 jit_solution(18149544916645652543)
XLA Ops:
  0.0 0.0 copy-start.4
  0.0 0.0 copy-start.5
  0.0 0.7 %copy-done.4 = s32[1,4,64]{2,1,0:T(4,128)S(1)} copy-done((s32[1,4,64]{2,1,0:T(4,128)S(1)}, s32[1,4,64]{2,1,0:T(4,128)}, u32[]{:S(2)}) %copy-start.4) | copy-done | bytes 1048
  0.7 0.0 copy-done.5
  0.7 0.0 copy-start.3
  0.7 0.0 copy-start
  0.7 0.0 copy-start.1
  0.7 1.6 %pack_blocks_and_strips.1 = (f32[192,128]{1,0:T(8,128)S(1)}, f32[112,128]{1,0:T(8,128)S(1)}, f32[192,128]{1,0:T(8,128)S(1)}) custom-call(s32[1,4]{1,0:T(1,128)S(1)} %copy-done.5, s32[4,64]{1,0:T(4,128)S(1)} %bitcast.19, f32[4,64,128]{2,1,0:T(8,128)} %bitcast.17, f32[4,128,128]{2,1,0:T(8,128)} %bitcast.10, f32[2,128,128]{2,1,0:T(8,128)} %bitcast.13, ...), custom_call_target="tpu_custom_call" | custom-call | tf_op jit(solution)/shard_map/pack_blocks_and_strips/pallas_call | solution.py:516
  2.3 0.0 copy-start.2
  2.3 3.6 %collective-permute-start = (f32[192,128]{1,0:T(8,128)S(1)}, f32[192,128]{1,0:T(8,128)S(1)}, u32[]{:S(2)}, u32[]{:S(2)}) collective-permute-start(f32[192,128]{1,0:T(8,128)S(1)} %get-tuple-element.14), channel_id=1, source_target_pairs={{0,3},{1,2},{2,1},{3,0},{4,7},{5,6},{6,5},{7,4},{8,11},{9,10},{10,... | collective-permute-start | bytes 294920 | tf_op jit(solution)/shard_map/ppermute | solution.py:534
  6.0 4.4 %collective-permute-start.2 = (f32[192,128]{1,0:T(8,128)S(1)}, f32[192,128]{1,0:T(8,128)S(1)}, u32[]{:S(2)}, u32[]{:S(2)}) collective-permute-start(f32[192,128]{1,0:T(8,128)S(1)} %get-tuple-element.16), channel_id=1, source_target_pairs={{0,1},{1,0},{2,3},{3,2},{4,5},{5,4},{6,7},{7,6},{8,9},{9,8},{10,11... | collective-permute-start | bytes 294920 | tf_op jit(solution)/shard_map/ppermute | solution.py:534
  10.4 1.9 %collective-permute-start.1 = (f32[112,128]{1,0:T(8,128)S(1)}, f32[112,128]{1,0:T(8,128)S(1)}, u32[]{:S(2)}, u32[]{:S(2)}) collective-permute-start(f32[112,128]{1,0:T(8,128)S(1)} %get-tuple-element.15), channel_id=1, source_target_pairs={{0,2},{1,3},{2,0},{3,1},{4,6},{5,7},{6,4},{7,5},{8,10},{9,11},{10,... | collective-permute-start | bytes 172040 | tf_op jit(solution)/shard_map/ppermute | solution.py:534
  12.3 0.0 copy-done.3
  12.3 0.8 %own_blocks.1.own_ref = f32[112,128]{1,0:T(8,128)S(1)} custom-call(s32[1,4]{1,0:T(1,128)S(1)} %copy-done.5, s32[4,64]{1,0:T(4,128)S(1)} %bitcast.20, f32[4,64,128]{2,1,0:T(8,128)S(1)} %bitcast.18), custom_call_target="tpu_custom_call" | custom-call | flops 5000000 | bytes 1000000 | tf_op jit(solution)/shard_map/own_blocks/pallas_call | solution.py:537
  13.1 4.2 %collective-permute-done.1.got2_ref = f32[112,128]{1,0:T(8,128)S(1)} collective-permute-done((f32[112,128]{1,0:T(8,128)S(1)}, f32[112,128]{1,0:T(8,128)S(1)}, u32[]{:S(2)}, u32[]{:S(2)}) %collective-permute-start.1) | collective-permute-done | bytes 57376 | tf_op jit(solution)/shard_map/ppermute | solution.py:534
  17.3 0.0 collective-permute-done.got3_ref
  17.3 0.0 collective-permute-done.2.got1_ref
  17.3 0.0 copy-done
  17.3 0.0 copy-done.1
  17.3 0.0 copy-done.2
  17.4 1.1 %scatter_and_halo.1 = (f32[400,128]{1,0:T(8,128)S(1)}, f32[400,128]{1,0:T(8,128)S(1)}, f32[8,128,128]{2,1,0:T(8,128)S(1)}, f32[128,128]{1,0:T(8,128)S(1)}) custom-call(f32[192,128]{1,0:T(8,128)S(1)} %collective-permute-done.got3_ref, f32[112,128]{1,0:T(8,128)S(1)} %collective-permute-done.1.got2_ref, f32[192,128]{1,0:T(8,128)S(1)} %collective-permute-done.2.got1_ref, ...), custom_call_target="tpu_custom_call" | custom-call | tf_op jit(solution)/shard_map/scatter_and_halo/pallas_call | solution.py:548
  18.4 6.2 %collective-permute-start.3 = (f32[400,128]{1,0:T(8,128)S(1)}, f32[400,128]{1,0:T(8,128)S(1)}, u32[]{:S(2)}, u32[]{:S(2)}) collective-permute-start(f32[400,128]{1,0:T(8,128)S(1)} %get-tuple-element.17.sent_odd_ref), channel_id=1, source_target_pairs={{4,8},{8,4},{12,16},{16,12},{20,24},{24,20},{28,32},{32,28},{36,40... | collective-permute-start | bytes 614408 | tf_op jit(solution)/shard_map/ppermute | solution.py:563
  24.6 1.9 %collective-permute-start.4 = (f32[400,128]{1,0:T(8,128)S(1)}, f32[400,128]{1,0:T(8,128)S(1)}, u32[]{:S(2)}, u32[]{:S(2)}) collective-permute-start(f32[400,128]{1,0:T(8,128)S(1)} %get-tuple-element.18.sent_even_ref), channel_id=1, source_target_pairs={{0,4},{4,0},{8,12},{12,8},{16,20},{20,16},{24,28},{28,24},{32,36},... | collective-permute-start | bytes 614408 | tf_op jit(solution)/shard_map/ppermute | solution.py:564
  26.5 1.8 %own_steps.1 = (f32[4,8,16,128]{3,2,1,0:T(8,128)S(1)}, f32[288,128]{1,0:T(8,128)S(1)}) custom-call(f32[8,128,128]{2,1,0:T(8,128)S(1)} %get-tuple-element.19.force_ref, f32[128,128]{1,0:T(8,128)S(1)} %get-tuple-element.20.strips_ref, f32[4,128,128]{2,1,0:T(8,128)S(1)} %bitcast.12, f32[2,128,128]{2,1,0:T(8,128)S(1)} %bitcast.15, f32[4,128,128]{2,1,0:T(8,128)S(1)} %bitcast.8), custom_call_target="tpu_custom_call" | custom-call | flops 10000000 | bytes 2000000 | tf_op jit(solution)/shard_map/own_steps/pallas_call | solution.py:566
  28.3 6.9 %collective-permute-done.3.odd_ref = f32[400,128]{1,0:T(8,128)S(1)} collective-permute-done((f32[400,128]{1,0:T(8,128)S(1)}, f32[400,128]{1,0:T(8,128)S(1)}, u32[]{:S(2)}, u32[]{:S(2)}) %collective-permute-start.3) | collective-permute-done | bytes 204832 | tf_op jit(solution)/shard_map/ppermute | solution.py:563
  35.2 0.0 collective-permute-done.4.even_ref
  35.2 1.7 %join_bands.1 = f32[4,128,128]{2,1,0:T(8,128)} custom-call(f32[400,128]{1,0:T(8,128)S(1)} %collective-permute-done.3.odd_ref, f32[400,128]{1,0:T(8,128)S(1)} %collective-permute-done.4.even_ref, f32[400,128]{1,0:T(8,128)S(1)} %get-tuple-element.17.sent_odd_ref, f32[400,128]{1,0:T(8,128)S(1)} %get-tuple-element.18.sent_even_ref, ...), custom_call_target="tpu_custom_call" | custom-call | tf_op jit(solution)/shard_map/join_bands/pallas_call | solution.py:576
Async XLA Ops:
  0.0 0.7 %copy-start.4 = (s32[1,4,64]{2,1,0:T(4,128)S(1)}, s32[1,4,64]{2,1,0:T(4,128)}, u32[]{:S(2)}) copy-start(s32[1,4,64]{2,1,0:T(4,128)} %param.10) | copy-start | bytes 3076
  0.0 0.7 %copy-start.5 = (s32[1,4]{1,0:T(1,128)S(1)}, s32[1,4]{1,0:T(1,128)}, u32[]{:S(2)}) copy-start(s32[1,4]{1,0:T(1,128)} %count_ref.1) | copy-start | bytes 52
  0.7 11.6 %copy-start.3 = (f32[1,4,64,128]{3,2,1,0:T(8,128)S(1)}, f32[1,4,64,128]{3,2,1,0:T(8,128)}, u32[]{:S(2)}) copy-start(f32[1,4,64,128]{3,2,1,0:T(8,128)} %param.9) | copy-start | bytes 393220
  0.7 16.6 %copy-start = (f32[4,16,8,128]{3,2,1,0:T(8,128)S(1)}, f32[4,16,8,128]{3,2,1,0:T(8,128)}, u32[]{:S(2)}) copy-start(f32[4,16,8,128]{3,2,1,0:T(8,128)} %param.8) | copy-start | bytes 786436
  0.7 16.6 %copy-start.1 = (f32[4,16,8,128]{3,2,1,0:T(8,128)S(1)}, f32[4,16,8,128]{3,2,1,0:T(8,128)}, u32[]{:S(2)}) copy-start(f32[4,16,8,128]{3,2,1,0:T(8,128)} %param.6) | copy-start | bytes 786436
  2.3 15.0 %copy-start.2 = (f32[2,16,8,128]{3,2,1,0:T(8,128)S(1)}, f32[2,16,8,128]{3,2,1,0:T(8,128)}, u32[]{:S(2)}) copy-start(f32[2,16,8,128]{3,2,1,0:T(8,128)} %param.7) | copy-start | bytes 393220
  2.3 15.0 %collective-permute-start = (f32[192,128]{1,0:T(8,128)S(1)}, f32[192,128]{1,0:T(8,128)S(1)}, u32[]{:S(2)}, u32[]{:S(2)}) collective-permute-start(f32[192,128]{1,0:T(8,128)S(1)} %get-tuple-element.14), channel_id=1, source_target_pairs={{0,3},{1,2},{2,1},{3,0},{4,7},{5,6},{6,5},{7,4},{8,11},{9,10},{10,... | collective-permute-start | bytes 294920 | tf_op jit(solution)/shard_map/ppermute | solution.py:534
  6.0 11.4 %collective-permute-start.2 = (f32[192,128]{1,0:T(8,128)S(1)}, f32[192,128]{1,0:T(8,128)S(1)}, u32[]{:S(2)}, u32[]{:S(2)}) collective-permute-start(f32[192,128]{1,0:T(8,128)S(1)} %get-tuple-element.16), channel_id=1, source_target_pairs={{0,1},{1,0},{2,3},{3,2},{4,5},{5,4},{6,7},{7,6},{8,9},{9,8},{10,11... | collective-permute-start | bytes 294920 | tf_op jit(solution)/shard_map/ppermute | solution.py:534
  10.4 7.0 %collective-permute-start.1 = (f32[112,128]{1,0:T(8,128)S(1)}, f32[112,128]{1,0:T(8,128)S(1)}, u32[]{:S(2)}, u32[]{:S(2)}) collective-permute-start(f32[112,128]{1,0:T(8,128)S(1)} %get-tuple-element.15), channel_id=1, source_target_pairs={{0,2},{1,3},{2,0},{3,1},{4,6},{5,7},{6,4},{7,5},{8,10},{9,11},{10,... | collective-permute-start | bytes 172040 | tf_op jit(solution)/shard_map/ppermute | solution.py:534
  18.4 16.8 %collective-permute-start.3 = (f32[400,128]{1,0:T(8,128)S(1)}, f32[400,128]{1,0:T(8,128)S(1)}, u32[]{:S(2)}, u32[]{:S(2)}) collective-permute-start(f32[400,128]{1,0:T(8,128)S(1)} %get-tuple-element.17.sent_odd_ref), channel_id=1, source_target_pairs={{4,8},{8,4},{12,16},{16,12},{20,24},{24,20},{28,32},{32,28},{36,40... | collective-permute-start | bytes 614408 | tf_op jit(solution)/shard_map/ppermute | solution.py:563
  24.6 10.6 %collective-permute-start.4 = (f32[400,128]{1,0:T(8,128)S(1)}, f32[400,128]{1,0:T(8,128)S(1)}, u32[]{:S(2)}, u32[]{:S(2)}) collective-permute-start(f32[400,128]{1,0:T(8,128)S(1)} %get-tuple-element.18.sent_even_ref), channel_id=1, source_target_pairs={{0,4},{4,0},{8,12},{12,8},{16,20},{20,16},{24,28},{28,24},{32,36},... | collective-permute-start | bytes 614408 | tf_op jit(solution)/shard_map/ppermute | solution.py:564

commit v4 on v3

--- a/solution.py
+++ b/solution.py
@@ -17,7 +17,15 @@
 LON_ROWS = 192
 
 A_AT, B_AT, C_AT, STRIP_AT = 16, 18, 19, 23
-LAT_ROWS = 25 * 16
+LAT_ROWS = 24 * 16
+SLOTS = {
+    **{field: (field * 8, 1, 6) for field in range(4)},
+    **{4 + field: (32 + field * 8, 2, 5) for field in range(4)},
+    **{8 + field: (112 + (field // 2) * 8 + (field % 2) * 2, 3, 4) for field in range(4)},
+    A_AT: (96, 1, 6),
+    B_AT: (104, 1, 6),
+    **{C_AT + field: (64 + field * 8, 2, 5) for field in range(4)},
+}
 CENTRE = 1.0 - 4.0 * DIFFUSION
 
 
@@ -104,8 +112,10 @@
             row += 8
 
 
-def strip_lane(plane, way):
-    return ((plane % 16) * 8 + way * (88 if plane == A_AT + 1 else 72)) % 128
+def slot_mask(plane, way, lane):
+    at, first, last = SLOTS[plane]
+    place = (lane - (at + way * 72)) & 127
+    return jnp.logical_and(place >= first, place <= last)
 
 
 def once(make):
@@ -277,14 +287,12 @@
         even_ref[at : at + 8, :] = jnp.where(is_even, up, down)
         odd_ref[at : at + 8, :] = jnp.where(is_even, down, up)
 
-    def put_strip(plane, packed, up_row, down_row):
+    def put_strip(plane, packed):
         for half in range(2):
-            for way, row in ((0, up_row), (1, down_row)):
-                at = strip_lane(plane, way)
-                mine = jnp.logical_and(lane >= at, lane < at + 8)
-                key = (STRIP_AT + plane // 16, half, way)
+            for way, row in ((0, 7), (1, 0)):
+                at = SLOTS[plane][0] + way * 72
                 moved = pltpu.roll(packed, (at - half * 64 - row * 8) % 128, 1)
-                sides[key] = jnp.where(mine, moved, sides.get(key, 0.0))
+                sides[half, way] = jnp.where(slot_mask(plane, way, lane), moved, sides.get((half, way), 0.0))
 
     def keep(step, u, strips):
         for field in range(4):
@@ -292,7 +300,7 @@
             for half in range(2):
                 put(plane, half, u[field][7, half], u[field][0, half])
             if step < 3:
-                put_strip(plane, strips[field], 7, 0)
+                put_strip(plane, strips[field])
 
     own_steps(
         lam_ref,
@@ -314,11 +322,11 @@
     ):
         for half in range(2):
             put(plane, half, levels(ref, field, 7 - depth, half * 8, 8), levels(ref, field, depth, half * 8, 8))
-        place = field + (4 if ref is winds_ref else 6)
-        put_strip(plane, strips_ref[place * 8 : place * 8 + 8, :], 7 - depth, depth)
-    for plane in (STRIP_AT, STRIP_AT + 1):
-        for half in range(2):
-            put(plane, half, sides[plane, half, 0], sides[plane, half, 1])
+        if depth == 0:
+            place = field + (4 if ref is winds_ref else 6)
+            put_strip(plane, strips_ref[place * 8 : place * 8 + 8, :])
+    for half in range(2):
+        put(STRIP_AT, half, sides[half, 0], sides[half, 1])
 
 
 def own_kernel(force_ref, strips_ref, lam_ref, winds_ref, coupling_ref, out_ref, wide_ref):
@@ -400,10 +408,8 @@
     couple = once(couple)
 
     def met(plane, half):
-        at = strip_lane(plane, 0)
-        mine = jnp.logical_and(lane >= at, lane < at + 8)
-        both = jnp.where(mine, low(STRIP_AT + plane // 16, half), high(STRIP_AT + plane // 16, half))
-        return pltpu.roll(both, ((0 if plane == A_AT + 1 else 8) - at) % 128, 1)
+        both = jnp.where(slot_mask(plane, 0, lane), low(STRIP_AT, half), high(STRIP_AT, half))
+        return pltpu.roll(both, (8 - SLOTS[plane][0]) % 128, 1)
 
     inside = jnp.logical_and(strip_row >= 0, strip_row <= 7)
 
@@ -415,10 +421,7 @@
         for half in range(2):
             at = (plane * 2 + half) * 8
             border_ref[at : at + 8, :] = strip(plane, plane, half)
-    deepest = jnp.logical_or(strip_row == -2, strip_row == 9)
-    strip_a = [
-        0.5 * jnp.where(deepest, met(A_AT + 1, half), strip(12, A_AT, half)) for half in range(2)
-    ]
+    strip_a = [0.5 * strip(12, A_AT, half) for half in range(2)]
     strip_b = [0.5 * strip(13, B_AT, half) for half in range(2)]
     strip_c = [[strip(14 + field, C_AT + field, half) for half in range(2)] for field in range(4)]
 

time: 37.2 us -> 37 us (level)
  no operation moved by 1% of the time
where the time goes in v4:
time: 37 us; the launch traced here: 36.8 us
  starting transfers between devices  18 us (49%)
  waiting for transfers between devices  11 us (30%)
  Pallas kernels  7 us (19%)
  local copies, waits for them, and re-layouts  0.7 us (2%)
    ppermute x3, starting transfers between devices, body(): lax.ppermute(parts[apart - 1], 'lon', [(i, i ^ apart) for i in range(tile...  9.92 us
    ppermute x1, waiting for transfers between devices, body(): got_odd = lax.ppermute(odd, 'lat', swap(1))  6.71 us
    ppermute x1, starting transfers between devices, body(): got_odd = lax.ppermute(odd, 'lat', swap(1))  6.16 us
    ppermute x3, waiting for transfers between devices, body(): lax.ppermute(parts[apart - 1], 'lon', [(i, i ^ apart) for i in range(tile...  4.25 us
    ppermute x1, starting transfers between devices, body(): got_even = lax.ppermute(even, 'lat', swap(0))  1.92 us
    pallas_call x1, Pallas kernels, body(): pl.pallas_call(own_kernel, out_shape=(jax.ShapeDtypeStruct((4, 8, 16, 128...  1.79 us
    pallas_call x1, Pallas kernels, body(): pl.pallas_call(functools.partial(join_kernel, bands), out_shape=jax.Shape...  1.73 us
    pallas_call x1, Pallas kernels, body(): pl.pallas_call(pack_kernel, out_shape=tuple((jax.ShapeDtypeStruct((rows,...  1.62 us
  transfers between devices with their start and end apart: 5, of which 2 were waited for; matrix products, arithmetic and copies ran while one was open for 0% of the time, Pallas kernels for 7%

profile of v4, /device:TPU:520, one launch (start us, length us, event | category | flops | bytes accessed | tf_op | source)
XLA Modules:
  0.0 36.8 jit_solution(5392847019523365901)
XLA Ops:
  0.0 0.0 copy-start.4
  0.0 0.0 copy-start.5
  0.0 0.7 %copy-done.4 = s32[1,4,64]{2,1,0:T(4,128)S(1)} copy-done((s32[1,4,64]{2,1,0:T(4,128)S(1)}, s32[1,4,64]{2,1,0:T(4,128)}, u32[]{:S(2)}) %copy-start.4) | copy-done | bytes 1048
  0.7 0.0 copy-done.5
  0.7 0.0 copy-start.3
  0.7 0.0 copy-start
  0.7 0.0 copy-start.1
  0.7 1.6 %pack_blocks_and_strips.1 = (f32[192,128]{1,0:T(8,128)S(1)}, f32[112,128]{1,0:T(8,128)S(1)}, f32[192,128]{1,0:T(8,128)S(1)}) custom-call(s32[1,4]{1,0:T(1,128)S(1)} %copy-done.5, s32[4,64]{1,0:T(4,128)S(1)} %bitcast.19, f32[4,64,128]{2,1,0:T(8,128)} %bitcast.17, f32[4,128,128]{2,1,0:T(8,128)} %bitcast.10, f32[2,128,128]{2,1,0:T(8,128)} %bitcast.13, ...), custom_call_target="tpu_custom_call" | custom-call | tf_op jit(solution)/shard_map/pack_blocks_and_strips/pallas_call | solution.py:519
  2.3 0.0 copy-start.2
  2.3 3.6 %collective-permute-start = (f32[192,128]{1,0:T(8,128)S(1)}, f32[192,128]{1,0:T(8,128)S(1)}, u32[]{:S(2)}, u32[]{:S(2)}) collective-permute-start(f32[192,128]{1,0:T(8,128)S(1)} %get-tuple-element.14), channel_id=1, source_target_pairs={{0,3},{1,2},{2,1},{3,0},{4,7},{5,6},{6,5},{7,4},{8,11},{9,10},{10,... | collective-permute-start | bytes 294920 | tf_op jit(solution)/shard_map/ppermute | solution.py:537
  6.0 4.4 %collective-permute-start.2 = (f32[192,128]{1,0:T(8,128)S(1)}, f32[192,128]{1,0:T(8,128)S(1)}, u32[]{:S(2)}, u32[]{:S(2)}) collective-permute-start(f32[192,128]{1,0:T(8,128)S(1)} %get-tuple-element.16), channel_id=1, source_target_pairs={{0,1},{1,0},{2,3},{3,2},{4,5},{5,4},{6,7},{7,6},{8,9},{9,8},{10,11... | collective-permute-start | bytes 294920 | tf_op jit(solution)/shard_map/ppermute | solution.py:537
  10.4 1.9 %collective-permute-start.1 = (f32[112,128]{1,0:T(8,128)S(1)}, f32[112,128]{1,0:T(8,128)S(1)}, u32[]{:S(2)}, u32[]{:S(2)}) collective-permute-start(f32[112,128]{1,0:T(8,128)S(1)} %get-tuple-element.15), channel_id=1, source_target_pairs={{0,2},{1,3},{2,0},{3,1},{4,6},{5,7},{6,4},{7,5},{8,10},{9,11},{10,... | collective-permute-start | bytes 172040 | tf_op jit(solution)/shard_map/ppermute | solution.py:537
  12.3 0.0 copy-done.3
  12.3 0.8 %own_blocks.1.own_ref = f32[112,128]{1,0:T(8,128)S(1)} custom-call(s32[1,4]{1,0:T(1,128)S(1)} %copy-done.5, s32[4,64]{1,0:T(4,128)S(1)} %bitcast.20, f32[4,64,128]{2,1,0:T(8,128)S(1)} %bitcast.18), custom_call_target="tpu_custom_call" | custom-call | flops 5000000 | bytes 1000000 | tf_op jit(solution)/shard_map/own_blocks/pallas_call | solution.py:540
  13.1 4.2 %collective-permute-done.1.got2_ref = f32[112,128]{1,0:T(8,128)S(1)} collective-permute-done((f32[112,128]{1,0:T(8,128)S(1)}, f32[112,128]{1,0:T(8,128)S(1)}, u32[]{:S(2)}, u32[]{:S(2)}) %collective-permute-start.1) | collective-permute-done | bytes 57376 | tf_op jit(solution)/shard_map/ppermute | solution.py:537
  17.3 0.0 collective-permute-done.got3_ref
  17.3 0.0 collective-permute-done.2.got1_ref
  17.3 0.0 copy-done
  17.3 0.0 copy-done.1
  17.3 0.0 copy-done.2
  17.4 1.1 %scatter_and_halo.1 = (f32[384,128]{1,0:T(8,128)S(1)}, f32[384,128]{1,0:T(8,128)S(1)}, f32[8,128,128]{2,1,0:T(8,128)S(1)}, f32[128,128]{1,0:T(8,128)S(1)}) custom-call(f32[192,128]{1,0:T(8,128)S(1)} %collective-permute-done.got3_ref, f32[112,128]{1,0:T(8,128)S(1)} %collective-permute-done.1.got2_ref, f32[192,128]{1,0:T(8,128)S(1)} %collective-permute-done.2.got1_ref, ...), custom_call_target="tpu_custom_call" | custom-call | tf_op jit(solution)/shard_map/scatter_and_halo/pallas_call | solution.py:551
  18.4 6.2 %collective-permute-start.3 = (f32[384,128]{1,0:T(8,128)S(1)}, f32[384,128]{1,0:T(8,128)S(1)}, u32[]{:S(2)}, u32[]{:S(2)}) collective-permute-start(f32[384,128]{1,0:T(8,128)S(1)} %get-tuple-element.17.sent_odd_ref), channel_id=1, source_target_pairs={{4,8},{8,4},{12,16},{16,12},{20,24},{24,20},{28,32},{32,28},{36,40... | collective-permute-start | bytes 589832 | tf_op jit(solution)/shard_map/ppermute | solution.py:566
  24.6 1.9 %collective-permute-start.4 = (f32[384,128]{1,0:T(8,128)S(1)}, f32[384,128]{1,0:T(8,128)S(1)}, u32[]{:S(2)}, u32[]{:S(2)}) collective-permute-start(f32[384,128]{1,0:T(8,128)S(1)} %get-tuple-element.18.sent_even_ref), channel_id=1, source_target_pairs={{0,4},{4,0},{8,12},{12,8},{16,20},{20,16},{24,28},{28,24},{32,36},... | collective-permute-start | bytes 589832 | tf_op jit(solution)/shard_map/ppermute | solution.py:567
  26.5 1.8 %own_steps.1 = (f32[4,8,16,128]{3,2,1,0:T(8,128)S(1)}, f32[288,128]{1,0:T(8,128)S(1)}) custom-call(f32[8,128,128]{2,1,0:T(8,128)S(1)} %get-tuple-element.19.force_ref, f32[128,128]{1,0:T(8,128)S(1)} %get-tuple-element.20.strips_ref, f32[4,128,128]{2,1,0:T(8,128)S(1)} %bitcast.12, f32[2,128,128]{2,1,0:T(8,128)S(1)} %bitcast.15, f32[4,128,128]{2,1,0:T(8,128)S(1)} %bitcast.8), custom_call_target="tpu_custom_call" | custom-call | flops 10000000 | bytes 2000000 | tf_op jit(solution)/shard_map/own_steps/pallas_call | solution.py:569
  28.3 6.7 %collective-permute-done.3.odd_ref = f32[384,128]{1,0:T(8,128)S(1)} collective-permute-done((f32[384,128]{1,0:T(8,128)S(1)}, f32[384,128]{1,0:T(8,128)S(1)}, u32[]{:S(2)}, u32[]{:S(2)}) %collective-permute-start.3) | collective-permute-done | bytes 196640 | tf_op jit(solution)/shard_map/ppermute | solution.py:566
  35.0 0.0 collective-permute-done.4.even_ref
  35.0 1.7 %join_bands.1 = f32[4,128,128]{2,1,0:T(8,128)} custom-call(f32[384,128]{1,0:T(8,128)S(1)} %collective-permute-done.3.odd_ref, f32[384,128]{1,0:T(8,128)S(1)} %collective-permute-done.4.even_ref, f32[384,128]{1,0:T(8,128)S(1)} %get-tuple-element.17.sent_odd_ref, f32[384,128]{1,0:T(8,128)S(1)} %get-tuple-element.18.sent_even_ref, ...), custom_call_target="tpu_custom_call" | custom-call | tf_op jit(solution)/shard_map/join_bands/pallas_call | solution.py:579
Async XLA Ops:
  0.0 0.7 %copy-start.4 = (s32[1,4,64]{2,1,0:T(4,128)S(1)}, s32[1,4,64]{2,1,0:T(4,128)}, u32[]{:S(2)}) copy-start(s32[1,4,64]{2,1,0:T(4,128)} %param.10) | copy-start | bytes 3076
  0.0 0.7 %copy-start.5 = (s32[1,4]{1,0:T(1,128)S(1)}, s32[1,4]{1,0:T(1,128)}, u32[]{:S(2)}) copy-start(s32[1,4]{1,0:T(1,128)} %count_ref.1) | copy-start | bytes 52
  0.7 11.6 %copy-start.3 = (f32[1,4,64,128]{3,2,1,0:T(8,128)S(1)}, f32[1,4,64,128]{3,2,1,0:T(8,128)}, u32[]{:S(2)}) copy-start(f32[1,4,64,128]{3,2,1,0:T(8,128)} %param.9) | copy-start | bytes 393220
  0.7 16.6 %copy-start = (f32[4,16,8,128]{3,2,1,0:T(8,128)S(1)}, f32[4,16,8,128]{3,2,1,0:T(8,128)}, u32[]{:S(2)}) copy-start(f32[4,16,8,128]{3,2,1,0:T(8,128)} %param.8) | copy-start | bytes 786436
  0.7 16.6 %copy-start.1 = (f32[4,16,8,128]{3,2,1,0:T(8,128)S(1)}, f32[4,16,8,128]{3,2,1,0:T(8,128)}, u32[]{:S(2)}) copy-start(f32[4,16,8,128]{3,2,1,0:T(8,128)} %param.6) | copy-start | bytes 786436
  2.3 15.0 %copy-start.2 = (f32[2,16,8,128]{3,2,1,0:T(8,128)S(1)}, f32[2,16,8,128]{3,2,1,0:T(8,128)}, u32[]{:S(2)}) copy-start(f32[2,16,8,128]{3,2,1,0:T(8,128)} %param.7) | copy-start | bytes 393220
  2.3 15.0 %collective-permute-start = (f32[192,128]{1,0:T(8,128)S(1)}, f32[192,128]{1,0:T(8,128)S(1)}, u32[]{:S(2)}, u32[]{:S(2)}) collective-permute-start(f32[192,128]{1,0:T(8,128)S(1)} %get-tuple-element.14), channel_id=1, source_target_pairs={{0,3},{1,2},{2,1},{3,0},{4,7},{5,6},{6,5},{7,4},{8,11},{9,10},{10,... | collective-permute-start | bytes 294920 | tf_op jit(solution)/shard_map/ppermute | solution.py:537
  6.0 11.4 %collective-permute-start.2 = (f32[192,128]{1,0:T(8,128)S(1)}, f32[192,128]{1,0:T(8,128)S(1)}, u32[]{:S(2)}, u32[]{:S(2)}) collective-permute-start(f32[192,128]{1,0:T(8,128)S(1)} %get-tuple-element.16), channel_id=1, source_target_pairs={{0,1},{1,0},{2,3},{3,2},{4,5},{5,4},{6,7},{7,6},{8,9},{9,8},{10,11... | collective-permute-start | bytes 294920 | tf_op jit(solution)/shard_map/ppermute | solution.py:537
  10.4 7.0 %collective-permute-start.1 = (f32[112,128]{1,0:T(8,128)S(1)}, f32[112,128]{1,0:T(8,128)S(1)}, u32[]{:S(2)}, u32[]{:S(2)}) collective-permute-start(f32[112,128]{1,0:T(8,128)S(1)} %get-tuple-element.15), channel_id=1, source_target_pairs={{0,2},{1,3},{2,0},{3,1},{4,6},{5,7},{6,4},{7,5},{8,10},{9,11},{10,... | collective-permute-start | bytes 172040 | tf_op jit(solution)/shard_map/ppermute | solution.py:537
  18.4 16.6 %collective-permute-start.3 = (f32[384,128]{1,0:T(8,128)S(1)}, f32[384,128]{1,0:T(8,128)S(1)}, u32[]{:S(2)}, u32[]{:S(2)}) collective-permute-start(f32[384,128]{1,0:T(8,128)S(1)} %get-tuple-element.17.sent_odd_ref), channel_id=1, source_target_pairs={{4,8},{8,4},{12,16},{16,12},{20,24},{24,20},{28,32},{32,28},{36,40... | collective-permute-start | bytes 589832 | tf_op jit(solution)/shard_map/ppermute | solution.py:566
  24.6 10.4 %collective-permute-start.4 = (f32[384,128]{1,0:T(8,128)S(1)}, f32[384,128]{1,0:T(8,128)S(1)}, u32[]{:S(2)}, u32[]{:S(2)}) collective-permute-start(f32[384,128]{1,0:T(8,128)S(1)} %get-tuple-element.18.sent_even_ref), channel_id=1, source_target_pairs={{0,4},{4,0},{8,12},{12,8},{16,20},{20,16},{24,28},{28,24},{32,36},... | collective-permute-start | bytes 589832 | tf_op jit(solution)/shard_map/ppermute | solution.py:567

commit v5 on v4

--- a/solution.py
+++ b/solution.py
@@ -225,7 +225,7 @@
 
 
 def halo_kernel(
-    got3_ref, got2_ref, got1_ref, own_ref, lam_ref, winds_ref, coupling_ref, even_ref, odd_ref, force_ref, strips_ref, edge_ref
+    got2_ref, got3_ref, got1_ref, own_ref, lam_ref, winds_ref, coupling_ref, even_ref, odd_ref, force_ref, strips_ref, edge_ref
 ):
     is_even = lax.rem(lax.axis_index("lat"), 2) == 0
     right_is_1 = lax.rem(lax.axis_index("lon"), 2) == 0
@@ -561,7 +561,7 @@
         scratch_shapes=[pltpu.VMEM((128, 128), F32)],
         compiler_params=params(),
         name="scatter_and_halo",
-    )(got3, got2, got1, own_part, lam, wind, couple)
+    )(got2, got3, got1, own_part, lam, wind, couple)
     swap = lambda first: [p for i in range(first, bands - 1, 2) for p in ((i, i + 1), (i + 1, i))]
     got_odd = lax.ppermute(odd, "lat", swap(1))
     got_even = lax.ppermute(even, "lat", swap(0))

time: 37 us -> 37 us (level)
  no operation moved by 1% of the time
where the time goes in v5:
time: 37 us; the launch traced here: 36.8 us
  starting transfers between devices  18 us (49%)
  waiting for transfers between devices  11 us (30%)
  Pallas kernels  6.99 us (19%)
  local copies, waits for them, and re-layouts  0.7 us (2%)
    ppermute x3, starting transfers between devices, body(): lax.ppermute(parts[apart - 1], 'lon', [(i, i ^ apart) for i in range(tile...  9.92 us
    ppermute x1, waiting for transfers between devices, body(): got_odd = lax.ppermute(odd, 'lat', swap(1))  6.71 us
    ppermute x1, starting transfers between devices, body(): got_odd = lax.ppermute(odd, 'lat', swap(1))  6.16 us
    ppermute x3, waiting for transfers between devices, body(): lax.ppermute(parts[apart - 1], 'lon', [(i, i ^ apart) for i in range(tile...  4.25 us
    ppermute x1, starting transfers between devices, body(): got_even = lax.ppermute(even, 'lat', swap(0))  1.92 us
    pallas_call x1, Pallas kernels, body(): pl.pallas_call(own_kernel, out_shape=(jax.ShapeDtypeStruct((4, 8, 16, 128...  1.79 us
    pallas_call x1, Pallas kernels, body(): pl.pallas_call(functools.partial(join_kernel, bands), out_shape=jax.Shape...  1.73 us
    pallas_call x1, Pallas kernels, body(): pl.pallas_call(pack_kernel, out_shape=tuple((jax.ShapeDtypeStruct((rows,...  1.62 us
  transfers between devices with their start and end apart: 5, of which 2 were waited for; matrix products, arithmetic and copies ran while one was open for 0% of the time, Pallas kernels for 7%

profile of v5, /device:TPU:520, one launch (start us, length us, event | category | flops | bytes accessed | tf_op | source)
XLA Modules:
  0.0 36.8 jit_solution(13311224921957929083)
XLA Ops:
  0.0 0.0 copy-start.4
  0.0 0.0 copy-start.5
  0.0 0.7 %copy-done.4 = s32[1,4,64]{2,1,0:T(4,128)S(1)} copy-done((s32[1,4,64]{2,1,0:T(4,128)S(1)}, s32[1,4,64]{2,1,0:T(4,128)}, u32[]{:S(2)}) %copy-start.4) | copy-done | bytes 1048
  0.7 0.0 copy-done.5
  0.7 0.0 copy-start.3
  0.7 0.0 copy-start
  0.7 0.0 copy-start.1
  0.7 1.6 %pack_blocks_and_strips.1 = (f32[192,128]{1,0:T(8,128)S(1)}, f32[112,128]{1,0:T(8,128)S(1)}, f32[192,128]{1,0:T(8,128)S(1)}) custom-call(s32[1,4]{1,0:T(1,128)S(1)} %copy-done.5, s32[4,64]{1,0:T(4,128)S(1)} %bitcast.19, f32[4,64,128]{2,1,0:T(8,128)} %bitcast.17, f32[4,128,128]{2,1,0:T(8,128)} %bitcast.10, f32[2,128,128]{2,1,0:T(8,128)} %bitcast.13, ...), custom_call_target="tpu_custom_call" | custom-call | tf_op jit(solution)/shard_map/pack_blocks_and_strips/pallas_call | solution.py:519
  2.3 0.0 copy-start.2
  2.3 3.6 %collective-permute-start.1 = (f32[192,128]{1,0:T(8,128)S(1)}, f32[192,128]{1,0:T(8,128)S(1)}, u32[]{:S(2)}, u32[]{:S(2)}) collective-permute-start(f32[192,128]{1,0:T(8,128)S(1)} %get-tuple-element.15), channel_id=1, source_target_pairs={{0,3},{1,2},{2,1},{3,0},{4,7},{5,6},{6,5},{7,4},{8,11},{9,10},{10,... | collective-permute-start | bytes 294920 | tf_op jit(solution)/shard_map/ppermute | solution.py:537
  6.0 4.4 %collective-permute-start.2 = (f32[192,128]{1,0:T(8,128)S(1)}, f32[192,128]{1,0:T(8,128)S(1)}, u32[]{:S(2)}, u32[]{:S(2)}) collective-permute-start(f32[192,128]{1,0:T(8,128)S(1)} %get-tuple-element.16), channel_id=1, source_target_pairs={{0,1},{1,0},{2,3},{3,2},{4,5},{5,4},{6,7},{7,6},{8,9},{9,8},{10,11... | collective-permute-start | bytes 294920 | tf_op jit(solution)/shard_map/ppermute | solution.py:537
  10.4 1.9 %collective-permute-start = (f32[112,128]{1,0:T(8,128)S(1)}, f32[112,128]{1,0:T(8,128)S(1)}, u32[]{:S(2)}, u32[]{:S(2)}) collective-permute-start(f32[112,128]{1,0:T(8,128)S(1)} %get-tuple-element.14), channel_id=1, source_target_pairs={{0,2},{1,3},{2,0},{3,1},{4,6},{5,7},{6,4},{7,5},{8,10},{9,11},{10,... | collective-permute-start | bytes 172040 | tf_op jit(solution)/shard_map/ppermute | solution.py:537
  12.3 0.0 copy-done.3
  12.3 0.8 %own_blocks.1.own_ref = f32[112,128]{1,0:T(8,128)S(1)} custom-call(s32[1,4]{1,0:T(1,128)S(1)} %copy-done.5, s32[4,64]{1,0:T(4,128)S(1)} %bitcast.20, f32[4,64,128]{2,1,0:T(8,128)S(1)} %bitcast.18), custom_call_target="tpu_custom_call" | custom-call | flops 5000000 | bytes 1000000 | tf_op jit(solution)/shard_map/own_blocks/pallas_call | solution.py:540
  13.1 4.2 %collective-permute-done.got2_ref = f32[112,128]{1,0:T(8,128)S(1)} collective-permute-done((f32[112,128]{1,0:T(8,128)S(1)}, f32[112,128]{1,0:T(8,128)S(1)}, u32[]{:S(2)}, u32[]{:S(2)}) %collective-permute-start) | collective-permute-done | bytes 57376 | tf_op jit(solution)/shard_map/ppermute | solution.py:537
  17.3 0.0 collective-permute-done.1.got3_ref
  17.3 0.0 collective-permute-done.2.got1_ref
  17.3 0.0 copy-done
  17.3 0.0 copy-done.1
  17.3 0.0 copy-done.2
  17.4 1.1 %scatter_and_halo.1 = (f32[384,128]{1,0:T(8,128)S(1)}, f32[384,128]{1,0:T(8,128)S(1)}, f32[8,128,128]{2,1,0:T(8,128)S(1)}, f32[128,128]{1,0:T(8,128)S(1)}) custom-call(f32[112,128]{1,0:T(8,128)S(1)} %collective-permute-done.got2_ref, f32[192,128]{1,0:T(8,128)S(1)} %collective-permute-done.1.got3_ref, f32[192,128]{1,0:T(8,128)S(1)} %collective-permute-done.2.got1_ref, ...), custom_call_target="tpu_custom_call" | custom-call | tf_op jit(solution)/shard_map/scatter_and_halo/pallas_call | solution.py:551
  18.4 6.2 %collective-permute-start.3 = (f32[384,128]{1,0:T(8,128)S(1)}, f32[384,128]{1,0:T(8,128)S(1)}, u32[]{:S(2)}, u32[]{:S(2)}) collective-permute-start(f32[384,128]{1,0:T(8,128)S(1)} %get-tuple-element.17.sent_odd_ref), channel_id=1, source_target_pairs={{4,8},{8,4},{12,16},{16,12},{20,24},{24,20},{28,32},{32,28},{36,40... | collective-permute-start | bytes 589832 | tf_op jit(solution)/shard_map/ppermute | solution.py:566
  24.6 1.9 %collective-permute-start.4 = (f32[384,128]{1,0:T(8,128)S(1)}, f32[384,128]{1,0:T(8,128)S(1)}, u32[]{:S(2)}, u32[]{:S(2)}) collective-permute-start(f32[384,128]{1,0:T(8,128)S(1)} %get-tuple-element.18.sent_even_ref), channel_id=1, source_target_pairs={{0,4},{4,0},{8,12},{12,8},{16,20},{20,16},{24,28},{28,24},{32,36},... | collective-permute-start | bytes 589832 | tf_op jit(solution)/shard_map/ppermute | solution.py:567
  26.5 1.8 %own_steps.1 = (f32[4,8,16,128]{3,2,1,0:T(8,128)S(1)}, f32[288,128]{1,0:T(8,128)S(1)}) custom-call(f32[8,128,128]{2,1,0:T(8,128)S(1)} %get-tuple-element.19.force_ref, f32[128,128]{1,0:T(8,128)S(1)} %get-tuple-element.20.strips_ref, f32[4,128,128]{2,1,0:T(8,128)S(1)} %bitcast.12, f32[2,128,128]{2,1,0:T(8,128)S(1)} %bitcast.15, f32[4,128,128]{2,1,0:T(8,128)S(1)} %bitcast.8), custom_call_target="tpu_custom_call" | custom-call | flops 10000000 | bytes 2000000 | tf_op jit(solution)/shard_map/own_steps/pallas_call | solution.py:569
  28.3 6.7 %collective-permute-done.3.odd_ref = f32[384,128]{1,0:T(8,128)S(1)} collective-permute-done((f32[384,128]{1,0:T(8,128)S(1)}, f32[384,128]{1,0:T(8,128)S(1)}, u32[]{:S(2)}, u32[]{:S(2)}) %collective-permute-start.3) | collective-permute-done | bytes 196640 | tf_op jit(solution)/shard_map/ppermute | solution.py:566
  35.0 0.0 collective-permute-done.4.even_ref
  35.0 1.7 %join_bands.1 = f32[4,128,128]{2,1,0:T(8,128)} custom-call(f32[384,128]{1,0:T(8,128)S(1)} %collective-permute-done.3.odd_ref, f32[384,128]{1,0:T(8,128)S(1)} %collective-permute-done.4.even_ref, f32[384,128]{1,0:T(8,128)S(1)} %get-tuple-element.17.sent_odd_ref, f32[384,128]{1,0:T(8,128)S(1)} %get-tuple-element.18.sent_even_ref, ...), custom_call_target="tpu_custom_call" | custom-call | tf_op jit(solution)/shard_map/join_bands/pallas_call | solution.py:579
Async XLA Ops:
  0.0 0.7 %copy-start.4 = (s32[1,4,64]{2,1,0:T(4,128)S(1)}, s32[1,4,64]{2,1,0:T(4,128)}, u32[]{:S(2)}) copy-start(s32[1,4,64]{2,1,0:T(4,128)} %param.10) | copy-start | bytes 3076
  0.0 0.7 %copy-start.5 = (s32[1,4]{1,0:T(1,128)S(1)}, s32[1,4]{1,0:T(1,128)}, u32[]{:S(2)}) copy-start(s32[1,4]{1,0:T(1,128)} %count_ref.1) | copy-start | bytes 52
  0.7 11.6 %copy-start.3 = (f32[1,4,64,128]{3,2,1,0:T(8,128)S(1)}, f32[1,4,64,128]{3,2,1,0:T(8,128)}, u32[]{:S(2)}) copy-start(f32[1,4,64,128]{3,2,1,0:T(8,128)} %param.9) | copy-start | bytes 393220
  0.7 16.6 %copy-start = (f32[4,16,8,128]{3,2,1,0:T(8,128)S(1)}, f32[4,16,8,128]{3,2,1,0:T(8,128)}, u32[]{:S(2)}) copy-start(f32[4,16,8,128]{3,2,1,0:T(8,128)} %param.8) | copy-start | bytes 786436
  0.7 16.6 %copy-start.1 = (f32[4,16,8,128]{3,2,1,0:T(8,128)S(1)}, f32[4,16,8,128]{3,2,1,0:T(8,128)}, u32[]{:S(2)}) copy-start(f32[4,16,8,128]{3,2,1,0:T(8,128)} %param.6) | copy-start | bytes 786436
  2.3 15.0 %copy-start.2 = (f32[2,16,8,128]{3,2,1,0:T(8,128)S(1)}, f32[2,16,8,128]{3,2,1,0:T(8,128)}, u32[]{:S(2)}) copy-start(f32[2,16,8,128]{3,2,1,0:T(8,128)} %param.7) | copy-start | bytes 393220
  2.3 15.0 %collective-permute-start.1 = (f32[192,128]{1,0:T(8,128)S(1)}, f32[192,128]{1,0:T(8,128)S(1)}, u32[]{:S(2)}, u32[]{:S(2)}) collective-permute-start(f32[192,128]{1,0:T(8,128)S(1)} %get-tuple-element.15), channel_id=1, source_target_pairs={{0,3},{1,2},{2,1},{3,0},{4,7},{5,6},{6,5},{7,4},{8,11},{9,10},{10,... | collective-permute-start | bytes 294920 | tf_op jit(solution)/shard_map/ppermute | solution.py:537
  6.0 11.4 %collective-permute-start.2 = (f32[192,128]{1,0:T(8,128)S(1)}, f32[192,128]{1,0:T(8,128)S(1)}, u32[]{:S(2)}, u32[]{:S(2)}) collective-permute-start(f32[192,128]{1,0:T(8,128)S(1)} %get-tuple-element.16), channel_id=1, source_target_pairs={{0,1},{1,0},{2,3},{3,2},{4,5},{5,4},{6,7},{7,6},{8,9},{9,8},{10,11... | collective-permute-start | bytes 294920 | tf_op jit(solution)/shard_map/ppermute | solution.py:537
  10.4 7.0 %collective-permute-start = (f32[112,128]{1,0:T(8,128)S(1)}, f32[112,128]{1,0:T(8,128)S(1)}, u32[]{:S(2)}, u32[]{:S(2)}) collective-permute-start(f32[112,128]{1,0:T(8,128)S(1)} %get-tuple-element.14), channel_id=1, source_target_pairs={{0,2},{1,3},{2,0},{3,1},{4,6},{5,7},{6,4},{7,5},{8,10},{9,11},{10,... | collective-permute-start | bytes 172040 | tf_op jit(solution)/shard_map/ppermute | solution.py:537
  18.4 16.6 %collective-permute-start.3 = (f32[384,128]{1,0:T(8,128)S(1)}, f32[384,128]{1,0:T(8,128)S(1)}, u32[]{:S(2)}, u32[]{:S(2)}) collective-permute-start(f32[384,128]{1,0:T(8,128)S(1)} %get-tuple-element.17.sent_odd_ref), channel_id=1, source_target_pairs={{4,8},{8,4},{12,16},{16,12},{20,24},{24,20},{28,32},{32,28},{36,40... | collective-permute-start | bytes 589832 | tf_op jit(solution)/shard_map/ppermute | solution.py:566
  24.6 10.4 %collective-permute-start.4 = (f32[384,128]{1,0:T(8,128)S(1)}, f32[384,128]{1,0:T(8,128)S(1)}, u32[]{:S(2)}, u32[]{:S(2)}) collective-permute-start(f32[384,128]{1,0:T(8,128)S(1)} %get-tuple-element.18.sent_even_ref), channel_id=1, source_target_pairs={{0,4},{4,0},{8,12},{12,8},{16,20},{20,16},{24,28},{28,24},{32,36},... | collective-permute-start | bytes 589832 | tf_op jit(solution)/shard_map/ppermute | solution.py:567
